TPU v7x, 32 devices: a whole 2x2x4 slice. The times are simulated.
32 devices in a mesh: dp: 8 (over z, x), fsdp: 4 (over y, core).
Axes of the slice: x: 2, y: 2, z: 4, core: 2. Of those that a mesh axis runs over, the one named last changes fastest.
Arguments:
- tokens: bfloat16 [16384, 1024], P(('dp', 'fsdp')), may hold values from -6 to 6
- mask_positions: int32 [32, 80], P(('dp', 'fsdp')), may hold values from 0 to 511, as said below
- mask_counts: int32 [32], P(('dp', 'fsdp')), may hold values from 1 to 80, as said below
- replace_ids: int32 [32, 80], P(('dp', 'fsdp')), may hold values from 0 to 29
- cotangent: bfloat16 [16384, 1024], P(('dp', 'fsdp')), may hold values from -6 to 6
- replace_table: bfloat16 [30, 1024], replicated, may hold values from -6 to 6
- w_qkv: bfloat16 [1024, 3072], P('fsdp'), may hold values from -0.25 to 0.25
- b_qv: bfloat16 [2048], P('fsdp'), may hold values from -3 to 3
- w_out: bfloat16 [1024, 1024], P('fsdp'), may hold values from -0.75 to 0.75
- b_out: bfloat16 [1024], P('fsdp'), may hold values from -3 to 3
- norm1_gain: bfloat16 [1024], P('fsdp'), may hold values from 0.5 to 1.5
- norm1_bias: bfloat16 [1024], P('fsdp'), may hold values from -3 to 3
- w_up: bfloat16 [1024, 4096], P('fsdp'), may hold values from -0.1875 to 0.1875
- b_up: bfloat16 [4096], P('fsdp'), may hold values from -3 to 3
- w_down: bfloat16 [4096, 1024], P('fsdp'), may hold values from -0.09375 to 0.09375
- b_down: bfloat16 [1024], P('fsdp'), may hold values from -3 to 3
- norm2_gain: bfloat16 [1024], P('fsdp'), may hold values from 0.5 to 1.5
- norm2_bias: bfloat16 [1024], P('fsdp'), may hold values from -3 to 3
Outputs:
- final: bfloat16 [16384, 1024], P(('dp', 'fsdp'))
- token_grad: float32 [16384, 1024], P(('dp', 'fsdp'))
- table_grad: float32 [30, 1024], replicated
- w_qkv_grad: float32 [1024, 3072], P('fsdp')
- b_qv_grad: float32 [2048], P('fsdp')
- w_out_grad: float32 [1024, 1024], P('fsdp')
- b_out_grad: float32 [1024], P('fsdp')
- norm1_gain_grad: float32 [1024], P('fsdp')
- norm1_bias_grad: float32 [1024], P('fsdp')
- w_up_grad: float32 [1024, 4096], P('fsdp')
- b_up_grad: float32 [4096], P('fsdp')
- w_down_grad: float32 [4096, 1024], P('fsdp')
- b_down_grad: float32 [1024], P('fsdp')
- norm2_gain_grad: float32 [1024], P('fsdp')
- norm2_bias_grad: float32 [1024], P('fsdp')
Inputs may be any that keep to these rules, and one draw needn't show every extreme that they name: `mask_positions`: the 80 positions of one sequence are all different. `mask_counts`: some sequence uses all 80 slots.
All inputs are finite; a program needn't handle non-finite values.
Results may differ from a plain program's by a relative error of at most 0.035.
Values may be sent and summed in bfloat16 or wider, within the bound.
A program may use at most 168 MiB of HBM per device.

v0:
```python
import math

import jax
import jax.numpy as jnp
from jax import lax
from jax.sharding import PartitionSpec as P

HEADS = 16


EPSILON = 1e-05


def normalize(values, gain, shift):
    mean = jnp.mean(values, axis=-1, keepdims=True)
    centred = values - mean
    spread = jnp.mean(centred * centred, axis=-1, keepdims=True)
    return centred * lax.rsqrt(spread + EPSILON) * gain + shift


def gelu_exact(values):
    return jax.nn.gelu(values, approximate=False)


def outer_dot(left, right):
    return lax.dot_general(
        left, right, (((0,), (0,)), ((), ())), preferred_element_type=jnp.float32
    )


def back_dot(left, right):
    return lax.dot_general(
        left, right, (((1,), (1,)), ((), ())), preferred_element_type=jnp.float32
    )


def attention_mix(block):
    query, keyed, weighted_values = block
    scores = jnp.einsum("qhe,khe->hqk", query, keyed, preferred_element_type=jnp.float32)
    probs = jax.nn.softmax(scores, axis=-1).astype(jnp.bfloat16)
    return jnp.einsum("hqk,khe->qhe", probs, weighted_values, preferred_element_type=jnp.float32)


def attend_back(block):
    query, keyed, weighted_values, d_mixed = block
    scores = jnp.einsum("qhe,khe->hqk", query, keyed, preferred_element_type=jnp.float32)
    probs = jax.nn.softmax(scores, axis=-1)
    rounded = probs.astype(jnp.bfloat16)
    d_probs = jnp.einsum(
        "qhe,khe->hqk", d_mixed, weighted_values, preferred_element_type=jnp.float32
    )
    inner = jnp.sum(d_probs * probs, axis=-1, keepdims=True)
    d_scores = (probs * (d_probs - inner)).astype(jnp.bfloat16)
    d_query = jnp.einsum(
        "hqk,khe->qhe", d_scores, keyed, preferred_element_type=jnp.float32
    ).astype(jnp.bfloat16)
    d_keyed = jnp.einsum(
        "hqk,qhe->khe", d_scores, query, preferred_element_type=jnp.float32
    ).astype(jnp.bfloat16)
    d_valued = jnp.einsum(
        "hqk,qhe->khe", rounded, d_mixed, preferred_element_type=jnp.float32
    ).astype(jnp.bfloat16)
    return (d_query, d_keyed, d_valued)


def layer_parts(rows, full, seq_dev, length):
    (
        w_qkv,
        b_qv,
        w_out,
        b_out,
        gain_one,
        bias_one,
        w_up,
        b_up,
        w_down,
        b_down,
        gain_two,
        bias_two,
    ) = full
    width = rows.shape[1]
    head_dim = width // HEADS
    scale = 1.0 / math.sqrt(head_dim)
    reduced_rows = rows.astype(jnp.bfloat16)
    joined = jnp.dot(reduced_rows, w_qkv, preferred_element_type=jnp.float32)
    bias_all = b_qv.astype(jnp.float32)
    query = ((joined[:, :width] + bias_all[:width]) * scale).astype(jnp.bfloat16)
    keyed = joined[:, width : 2 * width].astype(jnp.bfloat16)
    weighted_values = (joined[:, 2 * width :] + bias_all[width:]).astype(jnp.bfloat16)
    heads_of = lambda t: t.reshape(seq_dev, length, HEADS, head_dim)
    heads = (heads_of(query), heads_of(keyed), heads_of(weighted_values))
    mixed = lax.map(attention_mix, heads).reshape(-1, width).astype(jnp.bfloat16)
    branch = jnp.dot(mixed, w_out, preferred_element_type=jnp.float32) + b_out.astype(jnp.float32)
    hidden, first_pull = jax.vjp(
        normalize, rows + branch, gain_one.astype(jnp.float32), bias_one.astype(jnp.float32)
    )
    hidden_low = hidden.astype(jnp.bfloat16)
    inner = jnp.dot(hidden_low, w_up, preferred_element_type=jnp.float32) + b_up.astype(jnp.float32)
    active, gelu_pull = jax.vjp(gelu_exact, inner)
    active_low = active.astype(jnp.bfloat16)
    output = jnp.dot(active_low, w_down, preferred_element_type=jnp.float32) + b_down.astype(
        jnp.float32
    )
    result, second_pull = jax.vjp(
        normalize, hidden + output, gain_two.astype(jnp.float32), bias_two.astype(jnp.float32)
    )
    saved = (
        reduced_rows,
        heads,
        mixed,
        hidden_low,
        active_low,
        first_pull,
        gelu_pull,
        second_pull,
        scale,
    )
    return (result, saved)


def layer_back(rows, upstream, full, seq_dev, length):
    (
        w_qkv,
        b_qv,
        w_out,
        b_out,
        gain_one,
        bias_one,
        w_up,
        b_up,
        w_down,
        b_down,
        gain_two,
        bias_two,
    ) = full
    result, saved = layer_parts(rows, full, seq_dev, length)
    (
        reduced_rows,
        heads,
        mixed,
        hidden_low,
        active_low,
        first_pull,
        gelu_pull,
        second_pull,
        scale,
    ) = saved
    width = rows.shape[1]
    d_sum, d_gain_two, d_bias_two = second_pull(upstream)
    d_output = d_sum.astype(jnp.bfloat16)
    d_w_down = outer_dot(active_low, d_output)
    d_b_down = jnp.sum(d_output.astype(jnp.float32), axis=0)
    d_active = back_dot(d_output, w_down)
    d_inner = gelu_pull(d_active)[0].astype(jnp.bfloat16)
    d_w_up = outer_dot(hidden_low, d_inner)
    d_b_up = jnp.sum(d_inner.astype(jnp.float32), axis=0)
    d_hidden = d_sum + back_dot(d_inner, w_up)
    d_mid, d_gain_one, d_bias_one = first_pull(d_hidden)
    d_branch = d_mid.astype(jnp.bfloat16)
    d_w_out = outer_dot(mixed, d_branch)
    d_b_out = jnp.sum(d_branch.astype(jnp.float32), axis=0)
    d_mixed = back_dot(d_branch, w_out).astype(jnp.bfloat16)
    d_heads = d_mixed.reshape(heads[0].shape)
    d_query, d_keyed, d_valued = lax.map(attend_back, (heads[0], heads[1], heads[2], d_heads))
    d_query = d_query.reshape(-1, width) * scale
    d_joined = jnp.concatenate(
        [d_query, d_keyed.reshape(-1, width), d_valued.reshape(-1, width)], axis=1
    )
    d_w_qkv = outer_dot(reduced_rows, d_joined)
    d_b_qv = jnp.concatenate(
        [
            jnp.sum(d_query.astype(jnp.float32), axis=0),
            jnp.sum(d_valued.reshape(-1, width).astype(jnp.float32), axis=0),
        ]
    )
    d_rows = d_mid + back_dot(d_joined, w_qkv)
    grads = (
        d_w_qkv,
        d_b_qv,
        d_w_out,
        d_b_out,
        d_gain_one,
        d_bias_one,
        d_w_up,
        d_b_up,
        d_w_down,
        d_b_down,
        d_gain_two,
        d_bias_two,
    )
    return (d_rows, grads)


def share_grads(grads):
    rows = (
        lax.psum_scatter(
            grads[0].astype(jnp.bfloat16), "fsdp", scatter_dimension=0, tiled=True
        ).astype(jnp.float32),
        lax.psum_scatter(
            grads[1].astype(jnp.bfloat16), "fsdp", scatter_dimension=0, tiled=True
        ).astype(jnp.float32),
        lax.psum_scatter(
            grads[2].astype(jnp.bfloat16), "fsdp", scatter_dimension=0, tiled=True
        ).astype(jnp.float32),
        lax.psum_scatter(
            grads[3].astype(jnp.bfloat16), "fsdp", scatter_dimension=0, tiled=True
        ).astype(jnp.float32),
        lax.psum_scatter(
            grads[4].astype(jnp.bfloat16), "fsdp", scatter_dimension=0, tiled=True
        ).astype(jnp.float32),
        lax.psum_scatter(
            grads[5].astype(jnp.bfloat16), "fsdp", scatter_dimension=0, tiled=True
        ).astype(jnp.float32),
        lax.psum_scatter(
            grads[6].astype(jnp.bfloat16), "fsdp", scatter_dimension=0, tiled=True
        ).astype(jnp.float32),
        lax.psum_scatter(
            grads[7].astype(jnp.bfloat16), "fsdp", scatter_dimension=0, tiled=True
        ).astype(jnp.float32),
        lax.psum_scatter(
            grads[8].astype(jnp.bfloat16), "fsdp", scatter_dimension=0, tiled=True
        ).astype(jnp.float32),
        lax.psum_scatter(
            grads[9].astype(jnp.bfloat16), "fsdp", scatter_dimension=0, tiled=True
        ).astype(jnp.float32),
        lax.psum_scatter(
            grads[10].astype(jnp.bfloat16), "fsdp", scatter_dimension=0, tiled=True
        ).astype(jnp.float32),
        lax.psum_scatter(
            grads[11].astype(jnp.bfloat16), "fsdp", scatter_dimension=0, tiled=True
        ).astype(jnp.float32),
    )
    return (
        lax.psum(rows[0].astype(jnp.bfloat16), "dp").astype(jnp.float32),
        lax.psum(rows[1].astype(jnp.bfloat16), "dp").astype(jnp.float32),
        lax.psum(rows[2].astype(jnp.bfloat16), "dp").astype(jnp.float32),
        lax.psum(rows[3].astype(jnp.bfloat16), "dp").astype(jnp.float32),
        lax.psum(rows[4].astype(jnp.bfloat16), "dp").astype(jnp.float32),
        lax.psum(rows[5].astype(jnp.bfloat16), "dp").astype(jnp.float32),
        lax.psum(rows[6].astype(jnp.bfloat16), "dp").astype(jnp.float32),
        lax.psum(rows[7].astype(jnp.bfloat16), "dp").astype(jnp.float32),
        lax.psum(rows[8].astype(jnp.bfloat16), "dp").astype(jnp.float32),
        lax.psum(rows[9].astype(jnp.bfloat16), "dp").astype(jnp.float32),
        lax.psum(rows[10].astype(jnp.bfloat16), "dp").astype(jnp.float32),
        lax.psum(rows[11].astype(jnp.bfloat16), "dp").astype(jnp.float32),
    )


def shards(
    tokens,
    mask_positions,
    mask_counts,
    replace_ids,
    cotangent,
    replace_table,
    w_qkv,
    b_qv,
    w_out,
    b_out,
    norm1_gain,
    norm1_bias,
    w_up,
    b_up,
    w_down,
    b_down,
    norm2_gain,
    norm2_bias,
):
    seq_dev = mask_counts.shape[0]
    width = tokens.shape[1]
    length = tokens.shape[0] // seq_dev
    slots = mask_positions.shape[1]

    def fetch():
        return (
            lax.all_gather(w_qkv, "fsdp", axis=0, tiled=True),
            lax.all_gather(b_qv, "fsdp", axis=0, tiled=True),
            lax.all_gather(w_out, "fsdp", axis=0, tiled=True),
            lax.all_gather(b_out, "fsdp", axis=0, tiled=True),
            lax.all_gather(norm1_gain, "fsdp", axis=0, tiled=True),
            lax.all_gather(norm1_bias, "fsdp", axis=0, tiled=True),
            lax.all_gather(w_up, "fsdp", axis=0, tiled=True),
            lax.all_gather(b_up, "fsdp", axis=0, tiled=True),
            lax.all_gather(w_down, "fsdp", axis=0, tiled=True),
            lax.all_gather(b_down, "fsdp", axis=0, tiled=True),
            lax.all_gather(norm2_gain, "fsdp", axis=0, tiled=True),
            lax.all_gather(norm2_bias, "fsdp", axis=0, tiled=True),
        )

    used = (jnp.arange(slots, dtype=jnp.int32)[None, :] < mask_counts[:, None]).astype(jnp.float32)
    places = jnp.arange(length, dtype=jnp.int32)
    position_onehot = (mask_positions[:, :, None] == places[None, None, :]).astype(
        jnp.float32
    ) * used[:, :, None]
    entries = jnp.arange(replace_table.shape[0], dtype=jnp.int32)
    vocab_hot = (replace_ids[:, :, None] == entries[None, None, :]).astype(jnp.bfloat16)
    chosen = jnp.einsum("smv,vd->smd", vocab_hot, replace_table, preferred_element_type=jnp.float32)
    placed = jnp.einsum(
        "fhg,fhr->fgr",
        position_onehot.astype(jnp.bfloat16),
        chosen.astype(jnp.bfloat16),
        preferred_element_type=jnp.float32,
    )
    keep = 1.0 - jnp.sum(position_onehot, axis=1)[:, :, None]
    start = (tokens.astype(jnp.float32).reshape(seq_dev, length, width) * keep + placed).reshape(
        -1, width
    )
    middle = layer_parts(start, fetch(), seq_dev, length)[0]
    final = layer_parts(middle, fetch(), seq_dev, length)[0]
    d_middle, grads_two = layer_back(
        middle, cotangent.astype(jnp.float32), fetch(), seq_dev, length
    )
    shared_two = share_grads(grads_two)
    initial_gradient, grads_one = layer_back(start, d_middle, fetch(), seq_dev, length)
    shared = jax.tree.map(jnp.add, shared_two, share_grads(grads_one))
    initial_gradient = initial_gradient.reshape(seq_dev, length, width)
    token_grad = (initial_gradient * keep).reshape(-1, width)
    selected_gradient = jnp.einsum(
        "uko,uob->ukb", position_onehot, initial_gradient, precision=lax.Precision.HIGHEST
    )
    d_table = jnp.einsum(
        "smv,smd->vd",
        vocab_hot.astype(jnp.float32),
        selected_gradient,
        precision=lax.Precision.HIGHEST,
    )
    table_grad = lax.psum(d_table, ("dp", "fsdp"))
    return (
        final.astype(jnp.bfloat16),
        token_grad,
        table_grad,
        shared[0],
        shared[1],
        shared[2],
        shared[3],
        shared[4],
        shared[5],
        shared[6],
        shared[7],
        shared[8],
        shared[9],
        shared[10],
        shared[11],
    )


def solution(mesh):
    in_specs = (
        P(("dp", "fsdp"), None),
        P(("dp", "fsdp"), None),
        P(("dp", "fsdp")),
        P(("dp", "fsdp"), None),
        P(("dp", "fsdp"), None),
        P(),
        P("fsdp", None),
        P("fsdp"),
        P("fsdp", None),
        P("fsdp"),
        P("fsdp"),
        P("fsdp"),
        P("fsdp", None),
        P("fsdp"),
        P("fsdp", None),
        P("fsdp"),
        P("fsdp"),
        P("fsdp"),
    )
    out_specs = (
        P(("dp", "fsdp"), None),
        P(("dp", "fsdp"), None),
        P(),
        P("fsdp", None),
        P("fsdp"),
        P("fsdp", None),
        P("fsdp"),
        P("fsdp"),
        P("fsdp"),
        P("fsdp", None),
        P("fsdp"),
        P("fsdp", None),
        P("fsdp"),
        P("fsdp"),
        P("fsdp"),
    )
    return jax.shard_map(shards, mesh=mesh, in_specs=in_specs, out_specs=out_specs, check_vma=False)
```

profile of v0, /device:TPU:0, one launch (start us, length us, event | category | flops | bytes accessed | tf_op | source)
XLA Modules:
  0.0 1396.9 jit_solution(16930807887664488702)
XLA Ops:
  69.4 8.4 fusion.116
  89.8 53.3 %all-gather.16.cloned.1.call-done = bf16[1024,4096]{1,0:T(8,128)(2,1)} async-done(((bf16[256,4096]{1,0:T(8,128)(2,1)}), bf16[1024,4096]{1,0:T(8,128)(2,1)}) %all-gather.16.cloned.1.call-update) | async-done | bytes 8388624 | tf_op jit(solution)/shard_map/all_gather | solution.py:282
  143.1 27.7 %multiply_convert_fusion.3 = (bf16[512,4096]{1,0:T(8,128)(2,1)}, f32[512,4096]{1,0:T(8,128)}, f32[512,4096]{1,0:T(8,128)}) fusion(f32[4096]{0:T(1024)S(1)} %convert_element_type.443, bf16[1024,4096]{1,0:T(8,128)(2,1)} %all-gather.16.cloned.1.call-done, f32[512,1024]{1,0:T(8,128)S(1)} %get-tuple-element.198, f32[1024]{0:T(1024)S(1)} %bitcast.178, ...), kind=kOutput, calls=%fused_computation.28 | convolution fusion | flops 4436000768 | bytes 31485952 | tf_op jit(solution)/shard_map/dot_general | solution.py:98
  170.8 32.0 %all-gather.18.cloned.1.call-done = bf16[4096,1024]{1,0:T(8,128)(2,1)} async-done(((bf16[1024,1024]{1,0:T(8,128)(2,1)}), bf16[4096,1024]{1,0:T(8,128)(2,1)}) %all-gather.18.cloned.1.call-update) | async-done | bytes 8388624 | tf_op jit(solution)/shard_map/all_gather | solution.py:284
  202.8 8.4 fusion.118
  222.6 8.8 fusion.119
  243.7 27.8 %multiply_convert_fusion.2 = (bf16[512,4096]{1,0:T(8,128)(2,1)S(1)}, f32[512,4096]{1,0:T(8,128)}, f32[512,4096]{1,0:T(8,128)}) fusion(f32[4096]{0:T(1024)S(1)} %convert_element_type.443, bf16[1024,4096]{1,0:T(8,128)(2,1)} %all-gather.16.cloned.1.call-done, f32[512,1024]{1,0:T(8,128)S(1)} %get-tuple-element.205, f32[512]{0:T(512)S(1)} %fusion.70, ...), kind=kOutput, calls=%fused_computation.14 | convolution fusion | flops 4436000768 | bytes 31485952 | tf_op jit(solution)/shard_map/dot_general | solution.py:98
  280.8 15.6 %fusion.105 = (bf16[4096]{0:T(1024)(128)(2,1)}, bf16[512,4096]{1,0:T(8,128)(2,1)}) fusion(f32[512,4096]{1,0:T(8,128)} %get-tuple-element.185, f32[512,4096]{1,0:T(8,128)} %get-tuple-element.206, f32[4096]{0:T(1024)S(1)} %convert_element_type.443, bf16[512,1024]{1,0:T(8,128)(2,1)S(1)} %get-tuple-element.165, ...), kind=kOutput, calls=%fused_computation.198 | convolution fusion | flops 4328517632 | bytes 30433280 | tf_op jit(solution)/shard_map/dot_general | solution.py:32
  296.4 9.5 multiply_reduce_fusion.4
  316.9 8.9 bitcast_reduce_fusion.1
  325.8 13.5 multiply_reduce_fusion.1
  358.2 8.8 multiply_reduce_fusion.2
  367.9 15.7 %fusion.106 = (bf16[4096]{0:T(1024)(128)(2,1)S(1)}, bf16[512,4096]{1,0:T(8,128)(2,1)}) fusion(f32[512,4096]{1,0:T(8,128)} %get-tuple-element.187, f32[512,4096]{1,0:T(8,128)} %get-tuple-element.199, f32[4096]{0:T(1024)S(1)} %convert_element_type.443, bf16[512,1024]{1,0:T(8,128)(2,1)S(1)} %get-tuple-element.167, ...), kind=kOutput, calls=%fused_computation.199 | convolution fusion | flops 4328517632 | bytes 30433280 | tf_op jit(solution)/shard_map/dot_general | solution.py:32
  383.6 8.9 multiply_reduce_fusion.3
  411.3 9.9 bitcast_reduce_fusion
  421.2 13.6 multiply_reduce_fusion
  438.7 9.7 multiply_convert_fusion
  455.6 8.6 convolution_convert_fusion.4
  465.8 9.2 convolution_convert_fusion.3
  476.2 9.0 convolution_convert_fusion.1
  486.8 9.2 convolution_convert_fusion.2
  497.2 10.0 convolution_convert_fusion
  507.3 44.7 %reduce-scatter.11.cloned.1.call-done = bf16[256,3072]{1,0:T(8,128)(2,1)} async-done(((bf16[1024,3072]{1,0:T(8,128)(2,1)}), bf16[256,3072]{1,0:T(8,128)(2,1)}) %reduce-scatter.11.cloned.1.call-update) | async-done | bytes 1572880 | tf_op jit(solution)/shard_map/reduce_scatter | solution.py:196
  552.1 74.3 %reduce-scatter.17.cloned.1.call-done = bf16[256,4096]{1,0:T(8,128)(2,1)} async-done(((bf16[1024,4096]{1,0:T(8,128)(2,1)}), bf16[256,4096]{1,0:T(8,128)(2,1)}) %reduce-scatter.17.cloned.1.call-update) | async-done | bytes 2097168 | tf_op jit(solution)/shard_map/reduce_scatter | solution.py:214
  626.4 74.4 %reduce-scatter.21.cloned.1.call-done = bf16[1024,1024]{1,0:T(8,128)(2,1)} async-done(((bf16[4096,1024]{1,0:T(8,128)(2,1)}), bf16[1024,1024]{1,0:T(8,128)(2,1)}) %reduce-scatter.21.cloned.1.call-update) | async-done | bytes 2097168 | tf_op jit(solution)/shard_map/reduce_scatter | solution.py:220
  700.8 74.3 %reduce-scatter.19.cloned.1.call-done = bf16[256,4096]{1,0:T(8,128)(2,1)} async-done(((bf16[1024,4096]{1,0:T(8,128)(2,1)}), bf16[256,4096]{1,0:T(8,128)(2,1)}) %reduce-scatter.19.cloned.1.call-update) | async-done | bytes 2097168 | tf_op jit(solution)/shard_map/reduce_scatter | solution.py:214
  775.1 74.4 %reduce-scatter.23.cloned.1.call-done = bf16[1024,1024]{1,0:T(8,128)(2,1)} async-done(((bf16[4096,1024]{1,0:T(8,128)(2,1)}), bf16[1024,1024]{1,0:T(8,128)(2,1)}) %reduce-scatter.23.cloned.1.call-update) | async-done | bytes 2097168 | tf_op jit(solution)/shard_map/reduce_scatter | solution.py:220
  853.3 10.7 all-reduce.18
  865.0 39.6 %all-reduce.16 = (bf16[512]{0:T(512)(128)(2,1)S(1)}, bf16[512]{0:T(512)(128)(2,1)S(1)}, bf16[256]{0:T(256)(128)(2,1)S(1)}, bf16[256]{0:T(256)(128)(2,1)S(1)}, bf...) all-reduce(bf16[512]{0:T(512)(128)(2,1)S(1)} %dynamic-slice.3, ...), channel_id=1, replica_groups=mesh['dp'=8,'fsdp'=4] {'dp'}, use_global_device_ids=true, to_apply=%region_35.36 | all-reduce | flops 6144 | bytes 24576 | tf_op jit(solution)/shard_map/psum | solution.py:235
  909.2 9.1 broadcast_multiply_fusion
  920.7 339.8 %all-reduce.24.cloned.1.call-done = (bf16[256,3072]{1,0:T(8,128)(2,1)}, bf16[256,3072]{1,0:T(8,128)(2,1)}, bf16[256,1024]{1,0:T(8,128)(2,1)}, bf16[256,1024]{1,0...) async-done(((bf16[256,3072]{1,0:T(8,128)(2,1)}, bf16[256,3072]{1,0:T(8,128)(2,1)}, ...) | async-done | bytes 12582928 | tf_op jit(solution)/shard_map/psum | solution.py:234
  1271.6 116.8 %all-reduce.22.cloned.1.call-done = f32[30,1024]{1,0:T(8,128)} async-done(((f32[30,1024]{1,0:T(8,128)}), f32[30,1024]{1,0:T(8,128)}) %all-reduce.22.cloned.1.call-update) | async-done | bytes 122896 | tf_op jit(solution)/shard_map/psum | solution.py:327
  (365 shorter events, 194.1 us)
Async XLA Ops:
  7.2 45.9 %copy-start = (bf16[30,1024]{1,0:T(8,128)(2,1)S(1)}, bf16[30,1024]{1,0:T(8,128)(2,1)}, u32[]{:S(2)}) copy-start(bf16[30,1024]{1,0:T(8,128)(2,1)} %param.23) | copy-start | bytes 184324
  7.3 40.5 %copy-start.74 = (bf16[1024]{0:T(1024)(128)(2,1)S(1)}, bf16[1024]{0:T(1024)(128)(2,1)}, u32[]{:S(2)}) copy-start(bf16[1024]{0:T(1024)(128)(2,1)} %param.31) | copy-start | bytes 6148
  7.3 45.7 %copy-start.67 = (s32[1,80]{1,0:T(1,128)S(1)}, s32[1,80]{1,0:T(1,128)}, u32[]{:S(2)}) copy-start(s32[1,80]{1,0:T(1,128)} %param.19) | copy-start | bytes 964
  7.3 45.8 %copy-start.79 = (s32[1,80]{1,0:T(1,128)S(1)}, s32[1,80]{1,0:T(1,128)}, u32[]{:S(2)}) copy-start(s32[1,80]{1,0:T(1,128)} %param.21) | copy-start | bytes 964
  7.3 45.8 %copy-start.29 = (bf16[512,1024]{1,0:T(8,128)(2,1)S(1)}, bf16[512,1024]{1,0:T(8,128)(2,1)}, u32[]{:S(2)}) copy-start(bf16[512,1024]{1,0:T(8,128)(2,1)} %param.18) | copy-start | bytes 3145732
  7.3 51.7 %all-gather.12.cloned.1.call-start = ((), (), s32[]{:S(2)}) async-start(), calls=%async_computation.8 | async-start | bytes 7864320 | tf_op jit(solution)/shard_map/all_gather | solution.py:276
  8.0 77.4 %all-gather.14.cloned.1.call-start = ((), (), s32[]{:S(2)}) async-start(), calls=%async_computation.9 | async-start | bytes 2621440 | tf_op jit(solution)/shard_map/all_gather | solution.py:278
  8.8 134.3 %all-gather.16.cloned.1.call-start = ((), (), s32[]{:S(2)}) async-start(), calls=%async_computation.10 | async-start | bytes 10485760 | tf_op jit(solution)/shard_map/all_gather | solution.py:282
  9.5 193.3 %all-gather.18.cloned.1.call-start = ((), (), s32[]{:S(2)}) async-start(), calls=%async_computation.11 | async-start | bytes 10485760 | tf_op jit(solution)/shard_map/all_gather | solution.py:284
  10.1 497.2 %reduce-scatter.13.cloned.1.call-start = ((), (), s32[]{:S(2)}) async-start(), calls=%async_computation.15 | async-start | bytes 2621440 | tf_op jit(solution)/shard_map/reduce_scatter | solution.py:202
  32.5 239.0 %copy-start.72 = (f32[4,1,256]{2,1,0:T(1,128)}, f32[4,1,256]{2,1,0:T(1,128)S(1)}, u32[]{:S(2)}) copy-start(f32[4,1,256]{2,1,0:T(1,128)S(1)} %convert_element_type.525) | copy-start | bytes 12292
  89.4 113.4 %copy-start.13 = (f32[512,1024]{1,0:T(8,128)}, f32[512,1024]{1,0:T(8,128)S(1)}, u32[]{:S(2)}) copy-start(f32[512,1024]{1,0:T(8,128)S(1)} %get-tuple-element.198) | copy-start | bytes 6291460
  89.4 113.4 %copy-start.44 = (f32[512]{0:T(512)}, f32[512]{0:T(512)S(1)}, u32[]{:S(2)}) copy-start(f32[512]{0:T(512)S(1)} %broadcast_multiply_fusion.4) | copy-start | bytes 6148
  89.8 81.0 %copy-start.50 = (f32[512]{0:T(512)}, f32[512]{0:T(512)S(1)}, u32[]{:S(2)}) copy-start(f32[512]{0:T(512)S(1)} %multiply_reduce_fusion.11) | copy-start | bytes 6148
  89.8 113.1 %copy-start.58 = (f32[512]{0:T(512)}, f32[512]{0:T(512)S(1)}, u32[]{:S(2)}) copy-start(f32[512]{0:T(512)S(1)} %fusion.68) | copy-start | bytes 6148
  220.1 96.7 %copy-start.8 = (bf16[512,1024]{0,1:T(8,128)(2,1)}, bf16[512,1024]{0,1:T(8,128)(2,1)S(1)}, u32[]{:S(2)}) copy-start(bf16[512,1024]{0,1:T(8,128)(2,1)S(1)} %copy.94) | copy-start | bytes 3145732
  220.7 96.2 %copy-start.4 = (bf16[512,1024]{0,1:T(8,128)(2,1)}, bf16[512,1024]{0,1:T(8,128)(2,1)S(1)}, u32[]{:S(2)}) copy-start(bf16[512,1024]{0,1:T(8,128)(2,1)S(1)} %copy.95) | copy-start | bytes 3145732
  243.3 62.6 %copy-start.16 = (f32[512,1024]{1,0:T(8,128)}, f32[512,1024]{1,0:T(8,128)S(1)}, u32[]{:S(2)}) copy-start(f32[512,1024]{1,0:T(8,128)S(1)} %get-tuple-element.205) | copy-start | bytes 6291460
  243.3 62.6 %copy-start.46 = (f32[512]{0:T(512)}, f32[512]{0:T(512)S(1)}, u32[]{:S(2)}) copy-start(f32[512]{0:T(512)S(1)} %broadcast_multiply_fusion.2) | copy-start | bytes 6148
  243.6 62.3 %copy-start.60 = (f32[512]{0:T(512)}, f32[512]{0:T(512)S(1)}, u32[]{:S(2)}) copy-start(f32[512]{0:T(512)S(1)} %fusion.70) | copy-start | bytes 6148
  358.1 149.2 %reduce-scatter.15.cloned.1.call-start = ((), (), s32[]{:S(2)}) async-start(), calls=%async_computation.16 | async-start | bytes 2621440 | tf_op jit(solution)/shard_map/reduce_scatter | solution.py:202
  398.4 108.9 %reduce-scatter.9.cloned.1.call-start = ((), (), s32[]{:S(2)}) async-start(), calls=%async_computation.13 | async-start | bytes 7864320 | tf_op jit(solution)/shard_map/reduce_scatter | solution.py:196
  406.5 145.6 %reduce-scatter.11.cloned.1.call-start = ((), (), s32[]{:S(2)}) async-start(), calls=%async_computation.14 | async-start | bytes 7864320 | tf_op jit(solution)/shard_map/reduce_scatter | solution.py:196
  464.2 162.2 %reduce-scatter.17.cloned.1.call-start = ((), (), s32[]{:S(2)}) async-start(), calls=%async_computation.17 | async-start | bytes 10485760 | tf_op jit(solution)/shard_map/reduce_scatter | solution.py:214
  475.0 225.8 %reduce-scatter.21.cloned.1.call-start = ((), (), s32[]{:S(2)}) async-start(), calls=%async_computation.19 | async-start | bytes 10485760 | tf_op jit(solution)/shard_map/reduce_scatter | solution.py:220
  485.2 289.9 %reduce-scatter.19.cloned.1.call-start = ((), (), s32[]{:S(2)}) async-start(), calls=%async_computation.18 | async-start | bytes 10485760 | tf_op jit(solution)/shard_map/reduce_scatter | solution.py:214
  496.0 353.5 %reduce-scatter.23.cloned.1.call-start = ((), (), s32[]{:S(2)}) async-start(), calls=%async_computation.20 | async-start | bytes 10485760 | tf_op jit(solution)/shard_map/reduce_scatter | solution.py:220
  507.2 753.3 %all-reduce.24.cloned.1.call-start = ((), (), s32[]{:S(2)}) async-start(), calls=%async_computation.21 | async-start | bytes 25165824 | tf_op jit(solution)/shard_map/psum | solution.py:234
  849.6 59.6 %copy-start.12 = (f32[512,1024]{1,0:T(8,128)S(1)}, f32[512,1024]{1,0:T(8,128)}, u32[]{:S(2)}) copy-start(f32[512,1024]{1,0:T(8,128)} %copy-done.11) | copy-start | bytes 6291460
  849.6 59.6 %copy-start.66 = (f32[512]{0:T(512)S(1)}, f32[512]{0:T(512)}, u32[]{:S(2)}) copy-start(f32[512]{0:T(512)} %copy-done.65) | copy-start | bytes 6148
  849.6 538.8 %all-reduce.22.cloned.1.call-start = ((), (), s32[]{:S(2)}) async-start(), calls=%async_computation.12 | async-start | bytes 262144 | tf_op jit(solution)/shard_map/psum | solution.py:327
  1264.8 125.2 %copy-start.1 = (bf16[30,1024]{1,0:T(8,128)(2,1)S(1)}, bf16[30,1024]{1,0:T(8,128)(2,1)}, u32[]{:S(2)}) copy-start(bf16[30,1024]{1,0:T(8,128)(2,1)} %param.23) | copy-start | bytes 184324
  (85 other events, 633.8 us)
Sparse Core Ops, SparseCore 0:
  9.7 49.2 all-gather.11
  60.6 22.5 all-gather.13
  84.8 58.2 all-gather.15
  144.5 58.2 all-gather.17
  358.2 31.4 reduce-scatter.12
  398.5 31.4 reduce-scatter.14
  432.6 58.3 reduce-scatter.8
  493.7 58.3 reduce-scatter.10
  554.7 71.7 reduce-scatter.16
  629.0 71.7 reduce-scatter.20
  703.4 71.6 reduce-scatter.18
  777.7 71.7 reduce-scatter.22
  855.1 405.3 all-reduce.23
  1267.4 120.9 all-reduce.21
where the time goes:
time: 1410 us; the launch traced here: 1400 us
  waiting for transfers between devices  892 us (63%)
  matrix products  316 us (22%)
  blocking collectives  92.2 us (7%)
  other arithmetic  45.8 us (3%)
  local copies, waits for them, and re-layouts  32 us (2%)
  between operations  18.3 us (1%)
    psum x1, waiting for transfers between devices, share_grads(): lax.psum(rows[0].astype(jnp.bfloat16), 'dp').astype(jnp.float32)  340 us
    reduce_scatter x2, waiting for transfers between devices, share_grads(): lax.psum_scatter(grads[8].astype(jnp.bfloat16), 'fsdp', scatter_dimension...  149 us
    reduce_scatter x2, waiting for transfers between devices, share_grads(): lax.psum_scatter(grads[6].astype(jnp.bfloat16), 'fsdp', scatter_dimension...  149 us
    psum x1, waiting for transfers between devices, shards(): table_grad = lax.psum(d_table, ('dp', 'fsdp'))  117 us
    dot_general x8, matrix products, back_dot(): lax.dot_general(left, right, (((1,), (1,)), ((), ())), preferred_element_...  74.3 us
    dot_general x8, matrix products, outer_dot(): lax.dot_general(left, right, (((0,), (0,)), ((), ())), preferred_element_...  59.1 us
    dot_general x2, matrix products, layer_parts(): jnp.dot(hidden_low, w_up, preferred_element_type=jnp.float32)  55.5 us
    all_gather x1, waiting for transfers between devices, fetch(): lax.all_gather(w_up, 'fsdp', axis=0, tiled=True)  53.3 us
  transfers between devices with their start and end apart: 14, of which 10 were waited for; matrix products, arithmetic and copies ran while one was open for 16% of the time, Pallas kernels for 0%

commit v1 on v0

v1 whole, which is shorter than its diff:
```python
import functools
import math

import jax
import jax.numpy as jnp
from jax import lax
from jax.experimental import pallas as pl
from jax.experimental.pallas import tpu as pltpu
from jax.sharding import PartitionSpec as P

HEADS = 16
EPSILON = 1e-05
BF = jnp.bfloat16
F32 = jnp.float32
MESH = pl.DeviceIdType.MESH


def log2(n):
    return n.bit_length() - 1

def entry_barrier(partners):
    barrier = pltpu.get_barrier_semaphore()
    for partner in partners:
        pl.semaphore_signal(barrier, inc=1, device_id=partner, device_id_type=MESH)
    pl.semaphore_wait(barrier, len(partners))

def bit_of(value, bit):
    return lax.rem(value // (1 << bit), 2)

def flip(value, bit):
    return value + (1 - 2 * bit_of(value, bit)) * (1 << bit)

def gather_kernel(ndp, nf, shapes, *refs):
    n = len(shapes)
    ins, small, outs, small_out = refs[:n], refs[n], refs[n + 1:2 * n + 1], refs[2 * n + 1]
    send, recv, local = refs[2 * n + 2:]
    dp, me = lax.axis_index("dp"), lax.axis_index("fsdp")
    fbits = log2(nf)
    sibling = (dp, flip(me, 0))
    outer = [(dp, flip(me, b)) for b in range(1, fbits)]
    near = [(flip(dp, 0), me), (flip(dp, 1), me)]
    others = [(dp, lax.rem(me + d, nf)) for d in range(1, nf)]
    entry_barrier(others + near)
    code = lax.rem(dp, 4)
    counter = [0]
    started = []
    arrived = []

    def push(src, dst, partner):
        k = counter[0]
        counter[0] += 1
        copy = pltpu.make_async_remote_copy(src, dst, send.at[k], recv.at[k], device_id=partner, device_id_type=MESH)
        copy.start()
        started.append(copy)
        arrived.append(False)
        return k

    def arrive(k):
        started[k].wait_recv()
        arrived[k] = True

    small_copies = []
    for d in range(1, nf):
        small_copies.append(push(small, small_out.at[me], (dp, lax.rem(me + d, nf))))
    own_small = pltpu.make_async_copy(small, small_out.at[me], local.at[n])
    own_small.start()
    own = [own_small]
    for i in range(n):
        r, c = shapes[i]
        copy = pltpu.make_async_copy(ins[i], outs[i].at[pl.ds(pl.multiple_of(me * r, r), r)], local.at[i])
        copy.start()
        own.append(copy)

    def place(i, f, k, half):
        r, c = shapes[i]
        q, w = r // 4, c // 2
        return outs[i].at[pl.ds(pl.multiple_of(f * r + k * q, 16), q), pl.ds(half * w, w)]

    items = [(i, h) for i in range(n) for h in range(2)]
    waits = {}

    def stage(t, s):
        i, half = items[t]
        r, c = shapes[i]
        q, w = r // 4, c // 2
        p1, p2 = (0, 1) if half == 0 else (1, 0)
        if s == 0:
            src = ins[i].at[pl.ds(pl.multiple_of(code * q, 16), q), pl.ds(half * w, w)]
            if fbits > 1:
                waits[t, "y", 1] = [(me, push(src, place(i, me, code, half), outer[0]))]
            whole = ins[i].at[:, pl.ds(half * w, w)]
            push(whole, outs[i].at[pl.ds(pl.multiple_of(me * r, r), r), pl.ds(half * w, w)], sibling)
            return
        if s < fbits - 1 + 1 and s >= 1:
            got = []
            for f, copy in waits.pop((t, "y", s)):
                arrive(copy)
                got.append(flip(f, s))
            known.setdefault(t, []).extend(got)
            if s < fbits - 1:
                nxt = []
                src = ins[i].at[pl.ds(pl.multiple_of(code * q, 16), q), pl.ds(half * w, w)]
                nxt.append((me, push(src, place(i, me, code, half), outer[s])))
                for f in known[t]:
                    nxt.append((f, push(place(i, f, code, half), place(i, f, code, half), outer[s])))
                waits[t, "y", s + 1] = nxt
            else:
                waits[t, "p1"] = [(f, push(place(i, f, code, half), place(i, f, code, half), near[p1])) for f in known[t]]
                waits[t, "p2a"] = [(f, push(place(i, f, code, half), place(i, f, code, half), near[p2])) for f in known[t]]
            for f in got:
                push(place(i, f, code, half), place(i, f, code, half), sibling)
            return
        if s == fbits:
            k = flip(code, p1)
            out = []
            for f, copy in waits.pop((t, "p1")):
                arrive(copy)
                out.append((f, push(place(i, f, k, half), place(i, f, k, half), near[p2])))
                push(place(i, f, k, half), place(i, f, k, half), sibling)
            waits[t, "p2b"] = out
            return
        if s == fbits + 1:
            k = flip(code, p2)
            for f, copy in waits.pop((t, "p2a")):
                arrive(copy)
                push(place(i, f, k, half), place(i, f, k, half), sibling)
            return
        if s == fbits + 2:
            k = flip(flip(code, p2), p1)
            for f, copy in waits.pop((t, "p2b")):
                arrive(copy)
                push(place(i, f, k, half), place(i, f, k, half), sibling)

    known = {}
    stages = fbits + 3
    ahead = 2
    for step in range(-ahead, len(items) + stages - 1):
        for s in range(stages - 1, -1, -1):
            t = step - s if s else step + ahead
            if 0 <= t < len(items):
                stage(t, s)
    for copy, seen in zip(started, arrived):
        copy.wait_send()
        if not seen:
            copy.wait_recv()
    for copy in own:
        copy.wait()


def gather_weights(ndp, nf, collective_id, shards, small):
    shapes = tuple(s.shape for s in shards)
    fbits = log2(nf)
    per_item = (nf // 2 - 1) * 3 + 1 + (nf // 2 - 1) * 4 + (nf // 2 - 1)
    copies = nf - 1 + 2 * len(shards) * per_item
    any_space = pl.BlockSpec(memory_space=pl.ANY)
    outs = pl.pallas_call(
        functools.partial(gather_kernel, ndp, nf, shapes),
        out_shape=[jax.ShapeDtypeStruct((nf * r, c), jnp.bfloat16) for r, c in shapes]
        + [jax.ShapeDtypeStruct((nf,) + small.shape, small.dtype)],
        in_specs=[any_space] * (len(shards) + 1),
        out_specs=[any_space] * (len(shards) + 1),
        scratch_shapes=[
            pltpu.SemaphoreType.DMA((copies,)),
            pltpu.SemaphoreType.DMA((copies,)),
            pltpu.SemaphoreType.DMA((len(shards) + 1,)),
        ],
        compiler_params=pltpu.CompilerParams(collective_id=collective_id, has_side_effects=True),
        name="gather_weights",
    )(*shards, small)
    return outs[:-1], outs[-1]


def cut_plan(rows, cols, bits):
    plan = []
    for _ in range(bits):
        if rows >= 32:
            rows //= 2
            plan.append((0, rows))
        else:
            cols //= 2
            plan.append((1, cols))
    return plan


def reduce_kernel(ndp, nf, shapes, chunks, *refs):
    n = len(shapes)
    ins, outs = refs[:n], refs[n : 2 * n]
    held, from_core = refs[2 * n : 2 * n + 2]
    rest = refs[2 * n + 2 :]
    fbits, dbits = log2(nf), log2(ndp)
    from_outer, rest = rest[: fbits - 1], rest[fbits - 1 :]
    from_near, rest = rest[:dbits], rest[dbits:]
    done, send, recv, local, store = rest
    dp, me = lax.axis_index("dp"), lax.axis_index("fsdp")
    core = lax.rem(me, 2)
    sibling = (dp, flip(me, 0))
    outer = [(dp, flip(me, b)) for b in range(1, fbits)]
    near = [(flip(dp, b), me) for b in range(dbits)]
    entry_barrier([sibling] + outer + near)
    half = nf // 2
    started = []
    state = {}

    def push(src, dst, partner):
        k = len(started)
        copy = pltpu.make_async_remote_copy(
            src, dst, send.at[k], recv.at[k], device_id=partner, device_id_type=MESH
        )
        copy.start()
        started.append([copy, False])
        return k

    def arrive(k):
        started[k][0].wait_recv()
        started[k][1] = True

    def window(j, block, at):
        (r0, rr), (c0, cc) = at
        return held.at[j, block, pl.ds(r0, rr), pl.ds(c0, cc)]

    def stage(j, s):
        i, r0, c0, rn, cn = chunks[j]
        plan = cut_plan(rn, cn, dbits)
        block_rows = shapes[i][0] // nf
        if s == 0:
            loads, sends = [], []
            for b in range(half):
                mine = ins[i].at[pl.ds(pl.multiple_of((2 * b + core) * block_rows + r0, 16), rn), pl.ds(c0, cn)]
                theirs = ins[i].at[pl.ds(pl.multiple_of((2 * b + 1 - core) * block_rows + r0, 16), rn), pl.ds(c0, cn)]
                copy = pltpu.make_async_copy(mine, held.at[j, b, pl.ds(0, rn), pl.ds(0, cn)], local.at[j * half + b])
                copy.start()
                loads.append(copy)
                sends.append(push(theirs, from_core.at[j, b, pl.ds(0, rn), pl.ds(0, cn)], sibling))
            state[j] = (loads, sends)
            return
        if s == 1:
            loads, sends = state[j]
            for b in range(half):
                loads[b].wait()
                arrive(sends[b])
            held[j, :, :rn, :cn] += from_core[j, :, :rn, :cn]
            state[j] = (0, half)
        elif s < fbits + 1:
            bit = fbits - (s - 1)
            k, lo, size = state[j]
            arrive(k)
            held[j, pl.ds(lo, size), :rn, :cn] += from_outer[bit - 1][j, :, :rn, :cn]
            state[j] = (lo, size)
        if 1 <= s < fbits:
            bit = fbits - s
            lo, size = state[j]
            size //= 2
            mine = bit_of(me, bit)
            keep, give = lo + mine * size, lo + (1 - mine) * size
            k = push(
                held.at[j, pl.ds(give, size), pl.ds(0, rn), pl.ds(0, cn)],
                from_outer[bit - 1].at[j, :, pl.ds(0, rn), pl.ds(0, cn)],
                outer[bit - 1],
            )
            state[j] = (k, keep, size)
            return
        first = fbits
        if first <= s <= first + dbits:
            b = s - first
            if b == 0:
                lo, _ = state[j]
                at = ((0, rn), (0, cn))
            else:
                k, lo, at, history = state[j]
                arrive(k)
                (ra, rr), (ca, cc) = at
                total = held[j, lo, pl.ds(ra, rr), pl.ds(ca, cc)] + from_near[b - 1][j, :rr, :cc]
                if b == dbits:
                    done[j, pl.ds(ra, rr), pl.ds(ca, cc)] = total
                else:
                    held[j, lo, pl.ds(ra, rr), pl.ds(ca, cc)] = total
            if b < dbits:
                (ra, rr), (ca, cc) = at
                axis, size = plan[b]
                mine = bit_of(dp, b)
                if axis == 0:
                    keep = ((al(ra + mine * size, 16), size), (ca, cc))
                    give = ((al(ra + (1 - mine) * size, 16), size), (ca, cc))
                else:
                    keep = ((ra, rr), (al(ca + mine * size, 128), size))
                    give = ((ra, rr), (al(ca + (1 - mine) * size, 128), size))
                k = push(
                    window(j, lo, give), from_near[b].at[j, pl.ds(0, keep[0][1]), pl.ds(0, keep[1][1])], near[b]
                )
                history = [] if b == 0 else state[j][3]
                state[j] = (k, lo, keep, history + [at])
                return
            _, _, at, history = state[j]
        if s == first + dbits:
            at, history = state[j][2], state[j][3]
        else:
            b = dbits - (s - first - dbits)
            k, at, history = state[j]
            arrive(k)
            at, history = history[-1], history[:-1]
        if history:
            b = len(history) - 1
            (ra, rr), (ca, cc) = at
            piece = done.at[j, pl.ds(ra, rr), pl.ds(ca, cc)]
            k = push(piece, piece, near[b])
            state[j] = (k, at, history)
        else:
            copy = pltpu.make_async_copy(done.at[j, pl.ds(0, rn), pl.ds(0, cn)], outs[i].at[pl.ds(r0, rn), pl.ds(c0, cn)], store.at[j])
            copy.start()
            stores.append(copy)

    stores = []
    stages = fbits + 2 * dbits + 1
    ahead = 2
    for step in range(-ahead, len(chunks) + stages - 1):
        for s in range(stages - 1, -1, -1):
            j = step - s if s else step + ahead
            if 0 <= j < len(chunks):
                stage(j, s)
    for copy, seen in started:
        copy.wait_send()
        if not seen:
            copy.wait_recv()
    for copy in stores:
        copy.wait()


def al(value, by):
    return value if isinstance(value, int) else pl.multiple_of(value, by)


def reduce_grads(ndp, nf, collective_id, grads):
    shapes = tuple(g.shape for g in grads)
    fbits, dbits = log2(nf), log2(ndp)
    chunks = tuple(
        (i, r0, c0, min(128, r // nf), min(1024, c))
        for i, (r, c) in enumerate(shapes)
        for c0 in range(0, c, min(1024, c))
        for r0 in range(0, r // nf, min(128, r // nf))
    )
    n, half = len(chunks), nf // 2
    rn, cn = max(c[3] for c in chunks), max(c[4] for c in chunks)
    sizes = [(0, 0)] * dbits
    for _, _, _, rr, cc in chunks:
        for b, (axis, size) in enumerate(cut_plan(rr, cc, dbits)):
            rr, cc = (size, cc) if axis == 0 else (rr, size)
            sizes[b] = max(sizes[b][0], rr), max(sizes[b][1], cc)
    copies = n * (half + fbits - 1 + 2 * dbits)
    any_space = pl.BlockSpec(memory_space=pl.ANY)
    return pl.pallas_call(
        functools.partial(reduce_kernel, ndp, nf, shapes, chunks),
        out_shape=[jax.ShapeDtypeStruct((r // nf, c), jnp.bfloat16) for r, c in shapes],
        in_specs=[any_space] * len(grads),
        out_specs=[any_space] * len(grads),
        scratch_shapes=[
            pltpu.VMEM((n, half, rn, cn), jnp.bfloat16),
            pltpu.VMEM((n, half, rn, cn), jnp.bfloat16),
        ]
        + [pltpu.VMEM((n, 1 << (b - 1), rn, cn), jnp.bfloat16) for b in range(1, fbits)]
        + [pltpu.VMEM((n,) + size, jnp.bfloat16) for size in sizes]
        + [
            pltpu.VMEM((n, rn, cn), jnp.bfloat16),
            pltpu.SemaphoreType.DMA((copies,)),
            pltpu.SemaphoreType.DMA((copies,)),
            pltpu.SemaphoreType.DMA((n * half,)),
            pltpu.SemaphoreType.DMA((n,)),
        ],
        compiler_params=pltpu.CompilerParams(
            collective_id=collective_id, has_side_effects=True, vmem_limit_bytes=56 * 1024 * 1024
        ),
        name="reduce_grads",
    )(*grads)


def dot(left, right):
    return jnp.dot(left, right, preferred_element_type=F32)


def back_dot(left, right):
    return lax.dot_general(left, right, (((1,), (1,)), ((), ())), preferred_element_type=F32)


def outer_dot(left, right):
    return lax.dot_general(left, right, (((0,), (0,)), ((), ())), preferred_element_type=F32)


def norm_forward(t, gain, shift):
    mean = jnp.mean(t, axis=-1, keepdims=True)
    centred = t - mean
    spread = jnp.mean(centred * centred, axis=-1, keepdims=True)
    inverse = lax.rsqrt(spread + EPSILON)
    unit = centred * inverse
    return unit * gain + shift, unit, inverse


def norm_back(g, unit, inverse, gain):
    d_gain = jnp.sum(g * unit, axis=0)
    d_shift = jnp.sum(g, axis=0)
    gg = g * gain
    m1 = jnp.mean(gg, axis=-1, keepdims=True)
    m2 = jnp.mean(gg * unit, axis=-1, keepdims=True)
    return (gg - m1 - unit * m2) * inverse, d_gain, d_shift


def attention(q, k, v, length):
    heads = lambda t: t.reshape(length, HEADS, -1)
    scores = jnp.einsum("qhe,khe->hqk", heads(q), heads(k), preferred_element_type=F32)
    probs = jax.nn.softmax(scores, axis=-1).astype(BF)
    mixed = jnp.einsum("hqk,khe->qhe", probs, heads(v), preferred_element_type=F32)
    return mixed.reshape(length, -1).astype(BF), probs


def attention_back(q, k, v, probs, mixed, d_mixed, length):
    heads = lambda t: t.reshape(length, HEADS, -1)
    qh, kh, vh, doh = heads(q), heads(k), heads(v), heads(d_mixed)
    d_probs = jnp.einsum("qhe,khe->hqk", doh, vh, preferred_element_type=F32)
    inner = jnp.einsum("qhe,qhe->hq", doh.astype(F32), heads(mixed).astype(F32))[:, :, None]
    d_scores = (probs.astype(F32) * (d_probs - inner)).astype(BF)
    dq = jnp.einsum("hqk,khe->qhe", d_scores, kh, preferred_element_type=F32).astype(BF)
    dk = jnp.einsum("hqk,qhe->khe", d_scores, qh, preferred_element_type=F32).astype(BF)
    dv = jnp.einsum("hqk,qhe->khe", probs, doh, preferred_element_type=F32).astype(BF)
    flat = lambda t: t.reshape(length, -1)
    return flat(dq), flat(dk), flat(dv)


def forward(rows, w, length):
    width = rows.shape[1]
    scale = 1.0 / math.sqrt(width // HEADS)
    low = rows.astype(BF)
    joined = dot(low, w["qkv"])
    q = ((joined[:, :width] + w["b_qv"][:width]) * scale).astype(BF)
    k = joined[:, width : 2 * width].astype(BF)
    v = (joined[:, 2 * width :] + w["b_qv"][width:]).astype(BF)
    mixed, probs = attention(q, k, v, length)
    branch = dot(mixed, w["out"]) + w["b_out"]
    hidden, unit1, inv1 = norm_forward(rows + branch, w["gain1"], w["bias1"])
    hidden_low = hidden.astype(BF)
    u = dot(hidden_low, w["up"]) + w["b_up"]
    below = 0.5 * (1.0 + lax.erf(u * math.sqrt(0.5)))
    active = (u * below).astype(BF)
    slope = (below + u * (math.sqrt(0.5 / math.pi) * jnp.exp(-0.5 * u * u))).astype(BF)
    f = dot(active, w["down"]) + w["b_down"]
    result, unit2, inv2 = norm_forward(hidden + f, w["gain2"], w["bias2"])
    return result, dict(
        low=low, q=q, k=k, v=v, mixed=mixed, probs=probs, unit1=unit1, inv1=inv1,
        hidden=hidden_low, active=active, slope=slope, unit2=unit2, inv2=inv2,
    )


def backward(g, kept, w, length):
    width = g.shape[1]
    scale = 1.0 / math.sqrt(width // HEADS)
    total = lambda t: jnp.sum(t.astype(F32), axis=0)
    d_hf, d_gain2, d_bias2 = norm_back(g, kept["unit2"], kept["inv2"], w["gain2"])
    df = d_hf.astype(BF)
    du = (back_dot(df, w["down"]) * kept["slope"].astype(F32)).astype(BF)
    gh = d_hf + back_dot(du, w["up"])
    d_xz, d_gain1, d_bias1 = norm_back(gh, kept["unit1"], kept["inv1"], w["gain1"])
    dz = d_xz.astype(BF)
    d_mixed = back_dot(dz, w["out"]).astype(BF)
    dq, dk, dv = attention_back(kept["q"], kept["k"], kept["v"], kept["probs"], kept["mixed"], d_mixed, length)
    dq = dq * BF(scale)
    d_joined = jnp.concatenate([dq, dk, dv], axis=1)
    d_rows = d_xz + back_dot(d_joined, w["qkv"])
    vectors = (
        jnp.concatenate([total(dq), total(dv)]), total(dz), d_gain1, d_bias1,
        total(du), total(df), d_gain2, d_bias2,
    )
    return d_rows, dict(df=df, du=du, dz=dz, d_joined=d_joined), vectors


def shards(ndp, nf, tokens, mask_positions, mask_counts, replace_ids, cotangent, replace_table,
           w_qkv, b_qv, w_out, b_out, norm1_gain, norm1_bias, w_up, b_up, w_down, b_down, norm2_gain, norm2_bias):
    length, width = tokens.shape
    slots = mask_positions.shape[1]
    vectors = (b_qv, b_out, norm1_gain, norm1_bias, b_up, b_down, norm2_gain, norm2_bias)
    lengths = [t.shape[0] for t in vectors]
    count = sum(lengths)
    lanes = -(-count // 2048) * 128
    packed = jnp.pad(jnp.concatenate(vectors), (0, 16 * lanes - count)).reshape(16, lanes)
    (qkv, out, up, down), small = gather_weights(ndp, nf, 0, [w_qkv, w_out, w_up, w_down], packed)
    small = small.reshape(nf, 16 * lanes)
    names = ("b_qv", "b_out", "gain1", "bias1", "b_up", "b_down", "gain2", "bias2")
    w = dict(qkv=qkv, out=out, up=up, down=down)
    at = 0
    for name, size in zip(names, lengths):
        w[name] = small[:, at : at + size].reshape(-1).astype(F32)
        at += size

    used = (jnp.arange(slots, dtype=jnp.int32) < mask_counts[0]).astype(F32)
    places = jnp.arange(length, dtype=jnp.int32)
    position_hot = (mask_positions[0][:, None] == places[None, :]).astype(F32) * used[:, None]
    entries = jnp.arange(replace_table.shape[0], dtype=jnp.int32)
    vocab_hot = (replace_ids[0][:, None] == entries[None, :]).astype(BF)
    row_hot = outer_dot(position_hot.astype(BF), vocab_hot).astype(BF)
    keep = 1.0 - jnp.sum(position_hot, axis=0)[:, None]
    start = tokens.astype(F32) * keep + dot(row_hot, replace_table)

    middle, kept_one = forward(start, w, length)
    final, kept_two = forward(middle, w, length)
    d_middle, two, vectors_two = backward(cotangent.astype(F32), kept_two, w, length)
    d_start, one, vectors_one = backward(d_middle, kept_one, w, length)
    token_grad = d_start * keep

    def weight(left, right):
        both = lambda a, b: jnp.concatenate([a, b], axis=0)
        return outer_dot(both(kept_one[left], kept_two[left]), both(one[right], two[right])).astype(BF)

    (g_down,) = reduce_grads(ndp, nf, 1, [weight("active", "df")])
    (g_up,) = reduce_grads(ndp, nf, 2, [weight("hidden", "du")])
    high = d_start.astype(BF)
    rest = d_start - high.astype(F32)
    mid = rest.astype(BF)
    d_table = outer_dot(row_hot, high) + outer_dot(row_hot, mid)
    table_rows = -(-replace_table.shape[0] // 16) * 16
    d_table = jnp.pad(d_table, ((0, table_rows - d_table.shape[0]), (0, 0))).astype(BF)
    vec = [a + b for a, b in zip(vectors_one, vectors_two)]
    pieces = jnp.concatenate([t.reshape(nf, -1) for t in vec], axis=1)
    vec_rows = 64 - table_rows
    pieces = jnp.pad(pieces, ((0, 0), (0, vec_rows * width - count))).astype(BF).reshape(nf, vec_rows, width)
    extra = jnp.concatenate([pieces, jnp.broadcast_to(d_table[None], (nf,) + d_table.shape)], axis=1).reshape(-1, width)
    g_out, g_qkv, g_extra = reduce_grads(ndp, nf, 3, [weight("mixed", "dz"), weight("low", "d_joined"), extra])
    table_grad = g_extra[vec_rows : vec_rows + replace_table.shape[0]].astype(F32)
    flat = g_extra[:vec_rows].reshape(-1).astype(F32)
    v = []
    at = 0
    for size in lengths:
        v.append(flat[at : at + size])
        at += size
    up32 = lambda t: t.astype(F32)
    return (
        final.astype(BF), token_grad, table_grad, up32(g_qkv), v[0], up32(g_out), v[1], v[2], v[3],
        up32(g_up), v[4], up32(g_down), v[5], v[6], v[7],
    )


def solution(mesh):
    both = P(("dp", "fsdp"))
    rows = P("fsdp")
    in_specs = (both,) * 5 + (P(),) + (rows,) * 12
    out_specs = (both, both, P()) + (rows,) * 12
    body = functools.partial(shards, mesh.shape["dp"], mesh.shape["fsdp"])
    return jax.shard_map(body, mesh=mesh, in_specs=in_specs, out_specs=out_specs, check_vma=False)
```

time: 1410 us -> 765 us (0.54)
  waiting for transfers between devices: 892 us -> 0 us
  Pallas kernels: 0 us -> 457 us
  matrix products: 316 us -> 214 us
  blocking collectives: 92.2 us -> 0 us
  between operations: 18.3 us -> 2.84 us
    pallas_call x0 -> x4, Pallas kernels: none -> 457 us  [the longest x3 261 us: reduce_grads(): pl.pallas_call(functools.partial(reduce_kernel, ndp, nf, shapes, chunks),...]
    psum x2 -> x0, waiting for transfers between devices: 457 us -> none  [the longest x1 340 us: share_grads(): lax.psum(rows[0].astype(jnp.bfloat16), 'dp').astype(jnp.float32)]
    reduce_scatter x8 -> x0, waiting for transfers between devices: 342 us -> none  [the longest x2 149 us: share_grads(): lax.psum_scatter(grads[8].astype(jnp.bfloat16), 'fsdp', scatter_dimension...]
    all_gather x4 -> x0, waiting for transfers between devices: 90.6 us -> none  [the longest x1 53.3 us: fetch(): lax.all_gather(w_up, 'fsdp', axis=0, tiled=True)]
    dot_general x21 -> x19, matrix products: 165 us -> 78.8 us  [the longest x9 41.3 us: dot(): return jnp.dot(left, right, preferred_element_type=F32)]
    all_gather x8 -> x0, blocking collectives: 41.9 us -> none  [the longest x1 6.01 us: fetch(): lax.all_gather(norm2_bias, 'fsdp', axis=0, tiled=True)]
    psum x1 -> x0, blocking collectives: 39.6 us -> none  [share_grads(): lax.psum(rows[1].astype(jnp.bfloat16), 'dp').astype(jnp.float32)]
    add x12 -> x0, other arithmetic: 15.6 us -> none  [shards(): shared = jax.tree.map(jnp.add, shared_two, share_grads(grads_one))]
  transfers between devices with their start and end apart: 14 -> 0, of which waited for: 10 -> 0; matrix products, arithmetic and copies ran while one was open for 16% -> 0% of each run, Pallas kernels for 0% -> 0%
where the time goes in v1:
time: 765 us; the launch traced here: 756 us
  Pallas kernels  457 us (60%)
  matrix products  214 us (28%)
  other arithmetic  48.4 us (6%)
  local copies, waits for them, and re-layouts  33.6 us (4%)
    pallas_call x3, Pallas kernels, reduce_grads(): pl.pallas_call(functools.partial(reduce_kernel, ndp, nf, shapes, chunks),...  261 us
    pallas_call x1, Pallas kernels, gather_weights(): pl.pallas_call(functools.partial(gather_kernel, ndp, nf, shapes), out_sha...  197 us
    dot_general x8, matrix products, back_dot(): lax.dot_general(left, right, (((1,), (1,)), ((), ())), preferred_element_...  68.4 us
    dot_general x7, matrix products, outer_dot(): lax.dot_general(left, right, (((0,), (0,)), ((), ())), preferred_element_...  48.7 us
    dot_general x9, matrix products, dot(): return jnp.dot(left, right, preferred_element_type=F32)  41.3 us
    unnamed x150, local copies, waits for them, and re-layouts  18.5 us
    sub x2, matrix products, attention(): probs = jax.nn.softmax(scores, axis=-1).astype(BF)  18.3 us

profile of v1, /device:TPU:0, one launch (start us, length us, event | category | flops | bytes accessed | tf_op | source)
XLA Modules:
  0.0 756.1 jit_solution(17897999521174914528)
XLA Ops:
  13.4 196.5 %gather_weights.1 = (bf16[1024,3072]{1,0:T(8,128)(2,1)}, bf16[1024,1024]{1,0:T(8,128)(2,1)}, bf16[1024,4096]{1,0:T(8,128)(2,1)}, bf16[4096,1024]{1,0:T(8,128)(2,1)}, bf16[4,16,256]{2,1,0:T(8,128)(2,1)}) custom-call(bf16[256,3072]{1,0:T(8,128)(2,1)} %refs_0_.1, bf16[256,1024]{1,0:T(8,128)(2,1)} %refs_1_.1, bf16[256,4096]{1,0:T(8,128)(2,1)} %refs_2_.1, ...), custom_call_target="tpu_custom_call" | custom-call | tf_op jit(solution)/shard_map/gather_weights/pallas_call | solution.py:156
  210.9 5.5 fusion.130
  221.2 8.3 %fusion.124 = (f32[16,512]{1,0:T(8,128)S(1)}, f32[16,512,512]{1,2,0:T(8,128)}) fusion(bf16[512,16,64]{0,2,1:T(8,128)(2,1)S(1)} %bitcast.163, bf16[512,16,64]{0,2,1:T(8,128)(2,1)S(1)} %bitcast.159), kind=kOutput, calls=%fused_computation.240 | convolution fusion | flops 545260032 | bytes 18907136 | tf_op jit(solution)/shard_map/sub | solution.py:408
  229.5 6.8 divide_convert_fusion.1
  243.9 7.8 %multiply_convert_fusion.5 = (bf16[512,4096]{1,0:T(8,128)(2,1)}, f32[512,4096]{1,0:T(8,128)}) fusion(f32[4096]{0:T(1024)S(1)} %bitcast.219, bf16[512,1024]{1,0:T(8,128)(2,1)S(1)} %fusion.89, bf16[1024,4096]{1,0:T(8,128)(2,1)S(1)} %bitcast.230), kind=kOutput, calls=%fused_computation.34 | convolution fusion | flops 4307550208 | bytes 22036480 | tf_op jit(solution)/shard_map/dot_general | solution.py:376
  251.7 6.7 fusion.126
  259.8 3.4 fusion.131
  270.4 9.9 %fusion.127 = (f32[16,512]{1,0:T(8,128)S(1)}, f32[16,512,512]{1,2,0:T(8,128)}) fusion(bf16[512,16,64]{0,2,1:T(8,128)(2,1)} %bitcast.165, bf16[512,16,64]{0,2,1:T(8,128)(2,1)} %bitcast.161), kind=kOutput, calls=%fused_computation.243 | convolution fusion | flops 545260032 | bytes 18907136 | tf_op jit(solution)/shard_map/sub | solution.py:408
  280.3 7.3 divide_convert_fusion
  295.4 7.1 multiply_convert_fusion.4
  302.5 4.8 fusion.129
  311.5 11.1 %convert_reduce_fusion = (f32[4096]{0:T(1024)S(1)}, bf16[512,4096]{1,0:T(8,128)(2,1)S(1)}) fusion(f32[512,4096]{1,0:T(8,128)} %get-tuple-element.92, f32[4096]{0:T(1024)S(1)} %bitcast.221, bf16[512,1024]{1,0:T(8,128)(2,1)S(1)} %get-tuple-element.48, bf16[4096,1024]{1,0:T(8,128)(2,1)} %get-tuple-element.27), kind=kOutput, calls=%fused_computation.28 | convolution fusion | flops 4326420480 | bytes 22052864 | tf_op jit(solution)/shard_map/dot_general | solution.py:380
  322.5 10.4 %multiply_reduce_fusion.1 = (f32[1024]{0:T(1024)S(1)}, f32[512]{0:T(512)S(1)}, f32[512]{0:T(512)S(1)}, f32[1024]{0:T(1024)S(1)}, f32[512,1024]{1,0:T(8,128)S(1)}) fusion(f32[512,1024]{1,0:T(8,128)S(1)} %get-tuple-element.90, f32[512]{0:T(512)S(1)} %add_rsqrt_fusion.1, f32[512]{0:T(512)S(1)} %broadcast_multiply_fusion.10, f32[1024]{0:T(1024)S(1)} %bitcast.193, ...), kind=kOutput, calls=%fused_computation.109 | convolution fusion | flops 4304401408 | bytes 19955712 | tf_op jit(solution)/shard_map/dot_general | solution.py:380
  341.4 7.1 convert_reduce_fusion.7
  348.5 5.1 multiply_convert_fusion.1
  353.7 3.6 convolution_convert_fusion.4
  359.0 10.1 %multiply_reduce_fusion = (f32[1024]{0:T(1024)S(1)}, f32[512]{0:T(512)S(1)}, f32[512]{0:T(512)S(1)}, f32[1024]{0:T(1024)S(1)}, f32[512,1024]{1,0:T(8,128)}) fusion(f32[512,1024]{1,0:T(8,128)} %copy-done.4, f32[512]{0:T(512)S(1)} %add_rsqrt_fusion.2, f32[512]{0:T(512)S(1)} %broadcast_multiply_fusion.11, f32[1024]{0:T(1024)S(1)} %bitcast.202, ...), kind=kOutput, calls=%fused_computation.106 | convolution fusion | flops 3235902464 | bytes 15749120 | tf_op jit(solution)/shard_map/dot_general | solution.py:380
  369.2 4.2 convert_reduce_fusion.4
  373.4 12.1 %convert_reduce_fusion.1 = (f32[4096]{0:T(1024)S(1)}, bf16[512,4096]{1,0:T(8,128)(2,1)}) fusion(f32[512,4096]{1,0:T(8,128)} %get-tuple-element.84, f32[4096]{0:T(1024)S(1)} %bitcast.222, bf16[512,1024]{1,0:T(8,128)(2,1)S(1)} %get-tuple-element.50, bf16[4096,1024]{1,0:T(8,128)(2,1)} %get-tuple-element.27), kind=kOutput, calls=%fused_computation.29 | convolution fusion | flops 4326420480 | bytes 22052864 | tf_op jit(solution)/shard_map/dot_general | solution.py:380
  385.5 12.7 %fusion.20.refs_0_ = bf16[4096,1024]{1,0:T(8,128)(2,1)} fusion(bf16[512,4096]{1,0:T(8,128)(2,1)S(1)} %copy-done.48, bf16[512,4096]{1,0:T(8,128)(2,1)S(1)} %copy-done.46, bf16[512,1024]{1,0:T(8,128)(2,1)S(1)} %copy-done.37, bf16[512,1024]{1,0:T(8,128)(2,1)S(1)} %get-tuple-element.50), kind=kOutput, calls=%fused_computation.36 | convolution fusion | flops 8615100416 | bytes 18874368 | tf_op jit(solution)/shard_map/dot_general | solution.py:384
  398.3 86.0 %reduce_grads.5 = bf16[1024,1024]{1,0:T(8,128)(2,1)} custom-call(bf16[4096,1024]{1,0:T(8,128)(2,1)} %fusion.20.refs_0_), custom_call_target="tpu_custom_call" | custom-call | tf_op jit(solution)/shard_map/reduce_grads/pallas_call | solution.py:350
  484.3 11.6 %multiply_reduce_fusion.2 = (f32[1024]{0:T(1024)S(1)}, f32[512]{0:T(512)S(1)}, f32[512]{0:T(512)S(1)}, f32[1024]{0:T(1024)S(1)}, f32[512,1024]{1,0:T(8,128)}) fusion(f32[512,1024]{1,0:T(8,128)S(1)} %get-tuple-element.82, f32[512]{0:T(512)S(1)} %add_rsqrt_fusion.3, f32[512]{0:T(512)S(1)} %broadcast_multiply_fusion.12, f32[1024]{0:T(1024)S(1)} %bitcast.195, ...), kind=kOutput, calls=%fused_computation.110 | convolution fusion | flops 4300207104 | bytes 18894848 | tf_op jit(solution)/shard_map/dot_general | solution.py:380
  496.0 11.3 %fusion.23.refs_0_ = bf16[1024,4096]{1,0:T(8,128)(2,1)} fusion(bf16[512,4096]{1,0:T(8,128)(2,1)S(1)} %copy-done.51, bf16[512,4096]{1,0:T(8,128)(2,1)S(1)} %copy-done.49, bf16[512,1024]{1,0:T(8,128)(2,1)S(1)} %copy-done.34, bf16[512,1024]{1,0:T(8,128)(2,1)S(1)} %copy-done.32), kind=kOutput, calls=%fused_computation.37 | convolution fusion | flops 8615100416 | bytes 18874368 | tf_op jit(solution)/shard_map/dot_general | solution.py:384
  507.3 83.9 %reduce_grads.4 = bf16[256,4096]{1,0:T(8,128)(2,1)} custom-call(bf16[1024,4096]{1,0:T(8,128)(2,1)} %fusion.23.refs_0_), custom_call_target="tpu_custom_call" | custom-call | tf_op jit(solution)/shard_map/reduce_grads/pallas_call | solution.py:350
  591.3 3.7 convert_reduce_fusion.6
  600.2 5.2 fusion.84.refs_0_
  605.7 7.1 convert_reduce_fusion.9
  612.8 5.1 multiply_convert_fusion
  618.0 3.6 convolution_convert_fusion.1
  623.2 8.4 %broadcast_multiply_fusion = (f32[512,1024]{1,0:T(8,128)}, f32[512,1024]{1,0:T(8,128)S(1)}) fusion(f32[512]{0:T(512)S(1)} %copy-done.41, f32[512,1024]{1,0:T(8,128)S(1)} %copy-done.25, bf16[1024,3072]{1,0:T(8,128)(2,1)} %get-tuple-element.23, bf16[512,1024]{0,1:T(8,128)(2,1)} %bitcast.180, bf16[512,1024]{0,1:T(8,128)(2,1)} %bitcast.182, ...), kind=kOutput, calls=%fused_computation.168 | convolution fusion | flops 3231711232 | bytes 15730688 | tf_op jit(solution)/shard_map/dot_general | solution.py:380
  631.6 18.0 %fusion.38.refs_1_ = bf16[1024,3072]{1,0:T(8,128)(2,1)} fusion(bf16[512,1024]{0,1:T(8,128)(2,1)} %bitcast.177, bf16[512,1024]{0,1:T(8,128)(2,1)} %bitcast.179, bf16[512,1024]{0,1:T(8,128)(2,1)S(1)} %bitcast.172, bf16[512,1024]{0,1:T(8,128)(2,1)} %bitcast.181, bf16[512,1024]{0,1:T(8,128)(2,1)} %bitcast.183, bf16[512,1024]{0,1:T(8,128)(2,1)S(1)} %bitcast.174, ...), kind=kOutput, calls=%fused_computation.50 | convolution fusion | flops 6487539712 | bytes 14680064 | tf_op jit(solution)/shard_map/dot_general | solution.py:384
  651.3 90.8 %reduce_grads.3 = (bf16[256,1024]{1,0:T(8,128)(2,1)}, bf16[256,3072]{1,0:T(8,128)(2,1)}, bf16[64,1024]{1,0:T(8,128)(2,1)}) custom-call(bf16[1024,1024]{1,0:T(8,128)(2,1)} %fusion.84.refs_0_, bf16[1024,3072]{1,0:T(8,128)(2,1)} %fusion.38.refs_1_, bf16[256,1024]{1,0:T(8,128)(2,1)} %bitcast.175), custom_call_target="tpu_custom_call" | custom-call | tf_op jit(solution)/shard_map/reduce_grads/pallas_call | solution.py:350
  (247 shorter events, 77.8 us)
Async XLA Ops:
  0.6 9.8 %copy-start = (bf16[30,1024]{1,0:T(8,128)(2,1)S(1)}, bf16[30,1024]{1,0:T(8,128)(2,1)}, u32[]{:S(2)}) copy-start(bf16[30,1024]{1,0:T(8,128)(2,1)} %param.23) | copy-start | bytes 184324
  2.1 11.3 %copy-start.40 = (f32[512]{0:T(512)}, f32[512]{0:T(512)S(1)}, u32[]{:S(2)}) copy-start(f32[512]{0:T(512)S(1)} %broadcast_subtract_fusion) | copy-start | bytes 6148
  13.4 197.4 %copy-start.35 = (bf16[512,1024]{1,0:T(8,128)(2,1)}, bf16[512,1024]{1,0:T(8,128)(2,1)S(1)}, u32[]{:S(2)}) copy-start(bf16[512,1024]{1,0:T(8,128)(2,1)S(1)} %get-tuple-element.77) | copy-start | bytes 3145732
  219.3 10.3 %copy-start.10 = (bf16[512,1024]{0,1:T(8,128)(2,1)}, bf16[512,1024]{0,1:T(8,128)(2,1)S(1)}, u32[]{:S(2)}) copy-start(bf16[512,1024]{0,1:T(8,128)(2,1)S(1)} %copy.79) | copy-start | bytes 3145732
  221.2 15.2 %copy-start.6 = (bf16[512,1024]{0,1:T(8,128)(2,1)}, bf16[512,1024]{0,1:T(8,128)(2,1)S(1)}, u32[]{:S(2)}) copy-start(bf16[512,1024]{0,1:T(8,128)(2,1)S(1)} %copy.77) | copy-start | bytes 3145732
  229.5 14.4 %slice-start = ((s8[8388608]{0:T(1024)(128)(4,1)}), s8[4194304]{0:T(1024)(128)(4,1)S(1)}, s32[]{:S(2)}) async-start(s8[8388608]{0:T(1024)(128)(4,1)} %bitcast.229), calls=%async_computation | async-start | bytes 8388608
  236.4 7.5 slice-start.1
  243.5 8.3 %slice-start.4 = ((s8[8388608]{0:T(1024)(128)(4,1)}), s8[4194304]{0:T(1024)(128)(4,1)S(1)}, s32[]{:S(2)}) async-start(s8[8388608]{0:T(1024)(128)(4,1)} %bitcast.233), calls=%async_computation.4 | async-start | bytes 8388608
  243.9 7.8 %copy-start.31 = (bf16[512,1024]{1,0:T(8,128)(2,1)}, bf16[512,1024]{1,0:T(8,128)(2,1)S(1)}, u32[]{:S(2)}) copy-start(bf16[512,1024]{1,0:T(8,128)(2,1)S(1)} %fusion.89) | copy-start | bytes 3145732
  243.9 7.8 %slice-start.5 = ((s8[8388608]{0:T(1024)(128)(4,1)}), s8[4194304]{0:T(1024)(128)(4,1)S(1)}, s32[]{:S(2)}) async-start(s8[8388608]{0:T(1024)(128)(4,1)} %bitcast.233), calls=%async_computation.5 | async-start | bytes 8388608
  243.9 15.8 %slice-start.8 = ((s8[6291456]{0:T(1024)(128)(4,1)}), s8[4194304]{0:T(1024)(128)(4,1)S(1)}, s32[]{:S(2)}) async-start(s8[6291456]{0:T(1024)(128)(4,1)} %bitcast.237), calls=%async_computation.8 | async-start | bytes 8388608
  251.7 8.0 %slice-start.9 = ((s8[6291456]{0:T(1024)(128)(4,1)}), s8[2097152]{0:T(1024)(128)(4,1)S(1)}, s32[]{:S(2)}) async-start(s8[6291456]{0:T(1024)(128)(4,1)} %bitcast.237), calls=%async_computation.9 | async-start | bytes 4194304
  270.4 17.2 %copy-start.8 = (bf16[512,1024]{0,1:T(8,128)(2,1)}, bf16[512,1024]{0,1:T(8,128)(2,1)S(1)}, u32[]{:S(2)}) copy-start(bf16[512,1024]{0,1:T(8,128)(2,1)S(1)} %copy.81) | copy-start | bytes 3145732
  280.3 15.0 %slice-start.2 = ((s8[8388608]{0:T(1024)(128)(4,1)}), s8[4194304]{0:T(1024)(128)(4,1)S(1)}, s32[]{:S(2)}) async-start(s8[8388608]{0:T(1024)(128)(4,1)} %bitcast.231), calls=%async_computation.2 | async-start | bytes 8388608
  287.6 7.7 %slice-start.3 = ((s8[8388608]{0:T(1024)(128)(4,1)}), s8[4194304]{0:T(1024)(128)(4,1)S(1)}, s32[]{:S(2)}) async-start(s8[8388608]{0:T(1024)(128)(4,1)} %bitcast.231), calls=%async_computation.3 | async-start | bytes 8388608
  294.5 8.0 %slice-start.6 = ((s8[8388608]{0:T(1024)(128)(4,1)}), s8[4194304]{0:T(1024)(128)(4,1)S(1)}, s32[]{:S(2)}) async-start(s8[8388608]{0:T(1024)(128)(4,1)} %bitcast.235), calls=%async_computation.6 | async-start | bytes 8388608
  295.3 7.2 copy-start.33
  295.4 7.2 slice-start.7
  311.5 11.1 %copy-start.36 = (bf16[512,1024]{1,0:T(8,128)(2,1)}, bf16[512,1024]{1,0:T(8,128)(2,1)S(1)}, u32[]{:S(2)}) copy-start(bf16[512,1024]{1,0:T(8,128)(2,1)S(1)} %get-tuple-element.48) | copy-start | bytes 3145732
  322.5 10.5 %copy-start.50 = (bf16[512,4096]{1,0:T(8,128)(2,1)}, bf16[512,4096]{1,0:T(8,128)(2,1)S(1)}, u32[]{:S(2)}) copy-start(bf16[512,4096]{1,0:T(8,128)(2,1)S(1)} %get-tuple-element.111) | copy-start | bytes 12582916
  341.4 7.1 copy-start.9
  358.8 10.3 %copy-start.23 = (bf16[16,64,512]{2,1,0:T(8,128)(2,1)}, bf16[16,64,512]{2,1,0:T(8,128)(2,1)S(1)}, u32[]{:S(2)}) copy-start(bf16[16,64,512]{2,1,0:T(8,128)(2,1)S(1)} %get-tuple-element.103) | copy-start | bytes 3145732
  373.4 12.2 %copy-start.37 = (bf16[512,1024]{1,0:T(8,128)(2,1)S(1)}, bf16[512,1024]{1,0:T(8,128)(2,1)}, u32[]{:S(2)}) copy-start(bf16[512,1024]{1,0:T(8,128)(2,1)} %copy-done.36) | copy-start | bytes 3145732
  373.4 12.2 %copy-start.46 = (bf16[512,4096]{1,0:T(8,128)(2,1)S(1)}, bf16[512,4096]{1,0:T(8,128)(2,1)}, u32[]{:S(2)}) copy-start(bf16[512,4096]{1,0:T(8,128)(2,1)} %get-tuple-element.83) | copy-start | bytes 12582916
  373.4 12.2 %copy-start.48 = (bf16[512,4096]{1,0:T(8,128)(2,1)S(1)}, bf16[512,4096]{1,0:T(8,128)(2,1)}, u32[]{:S(2)}) copy-start(bf16[512,4096]{1,0:T(8,128)(2,1)} %copy-done.47) | copy-start | bytes 12582916
  484.3 11.7 %copy-start.32 = (bf16[512,1024]{1,0:T(8,128)(2,1)S(1)}, bf16[512,1024]{1,0:T(8,128)(2,1)}, u32[]{:S(2)}) copy-start(bf16[512,1024]{1,0:T(8,128)(2,1)} %copy-done.31) | copy-start | bytes 3145732
  484.3 11.7 %copy-start.34 = (bf16[512,1024]{1,0:T(8,128)(2,1)S(1)}, bf16[512,1024]{1,0:T(8,128)(2,1)}, u32[]{:S(2)}) copy-start(bf16[512,1024]{1,0:T(8,128)(2,1)} %copy-done.33) | copy-start | bytes 3145732
  484.3 11.7 %copy-start.49 = (bf16[512,4096]{1,0:T(8,128)(2,1)S(1)}, bf16[512,4096]{1,0:T(8,128)(2,1)}, u32[]{:S(2)}) copy-start(bf16[512,4096]{1,0:T(8,128)(2,1)} %get-tuple-element.109) | copy-start | bytes 12582916
  484.3 11.7 %copy-start.51 = (bf16[512,4096]{1,0:T(8,128)(2,1)S(1)}, bf16[512,4096]{1,0:T(8,128)(2,1)}, u32[]{:S(2)}) copy-start(bf16[512,4096]{1,0:T(8,128)(2,1)} %copy-done.50) | copy-start | bytes 12582916
  605.7 7.1 copy-start.7
  623.2 8.4 %copy-start.24 = (bf16[16,64,512]{2,1,0:T(8,128)(2,1)S(1)}, bf16[16,64,512]{2,1,0:T(8,128)(2,1)}, u32[]{:S(2)}) copy-start(bf16[16,64,512]{2,1,0:T(8,128)(2,1)} %copy-done.23) | copy-start | bytes 3145732
  631.6 18.1 %copy-start.39 = (bf16[512,30]{0,1:T(8,128)(2,1)S(1)}, bf16[512,30]{0,1:T(8,128)(2,1)}, u32[]{:S(2)}) copy-start(bf16[512,30]{0,1:T(8,128)(2,1)} %copy-done.38) | copy-start | bytes 92164
  (30 other events, 99.2 us)

commit v2 on v1

--- a/solution.py
+++ b/solution.py
@@ -30,10 +30,15 @@
 def flip(value, bit):
     return value + (1 - 2 * bit_of(value, bit)) * (1 << bit)
 
+CUTS = 4
+
+
+SKEW = 2
 def gather_kernel(ndp, nf, shapes, *refs):
     n = len(shapes)
     ins, small, outs, small_out = refs[:n], refs[n], refs[n + 1:2 * n + 1], refs[2 * n + 1]
-    send, recv, local = refs[2 * n + 2:]
+    staged = refs[2 * n + 2 : 3 * n + 2]
+    send, recv, local = refs[3 * n + 2 :]
     dp, me = lax.axis_index("dp"), lax.axis_index("fsdp")
     fbits = log2(nf)
     sibling = (dp, flip(me, 0))
@@ -65,25 +70,26 @@
     own_small = pltpu.make_async_copy(small, small_out.at[me], local.at[n])
     own_small.start()
     own = [own_small]
+    loads = []
     for i in range(n):
         r, c = shapes[i]
-        copy = pltpu.make_async_copy(ins[i], outs[i].at[pl.ds(pl.multiple_of(me * r, r), r)], local.at[i])
+        copy = pltpu.make_async_copy(ins[i], staged[i], local.at[i])
         copy.start()
-        own.append(copy)
+        loads.append(copy)
 
     def place(i, f, k, half):
         r, c = shapes[i]
-        q, w = r // 4, c // 2
+        q, w = r // 4, c // CUTS
         return outs[i].at[pl.ds(pl.multiple_of(f * r + k * q, 16), q), pl.ds(half * w, w)]
 
-    items = [(i, h) for i in range(n) for h in range(2)]
+    items = [(i, h) for i in range(n) for h in range(CUTS)]
     waits = {}
 
     def stage(t, s):
         i, half = items[t]
         r, c = shapes[i]
-        q, w = r // 4, c // 2
-        p1, p2 = (0, 1) if half == 0 else (1, 0)
+        q, w = r // 4, c // CUTS
+        p1, p2 = (0, 1) if half % 2 == 0 else (1, 0)
         if s == 0:
             src = ins[i].at[pl.ds(pl.multiple_of(code * q, 16), q), pl.ds(half * w, w)]
             if fbits > 1:
@@ -134,9 +140,16 @@
     known = {}
     stages = fbits + 3
     ahead = 2
-    for step in range(-ahead, len(items) + stages - 1):
+    for step in range(-ahead, len(items) + SKEW * (stages - 1)):
+        if step == 0:
+            for i in range(n):
+                r = shapes[i][0]
+                loads[i].wait()
+                copy = pltpu.make_async_copy(staged[i], outs[i].at[pl.ds(pl.multiple_of(me * r, r), r)], local.at[i])
+                copy.start()
+                own.append(copy)
         for s in range(stages - 1, -1, -1):
-            t = step - s if s else step + ahead
+            t = step - SKEW * s if s else step + ahead
             if 0 <= t < len(items):
                 stage(t, s)
     for copy, seen in zip(started, arrived):
@@ -151,7 +164,7 @@
     shapes = tuple(s.shape for s in shards)
     fbits = log2(nf)
     per_item = (nf // 2 - 1) * 3 + 1 + (nf // 2 - 1) * 4 + (nf // 2 - 1)
-    copies = nf - 1 + 2 * len(shards) * per_item
+    copies = nf - 1 + CUTS * len(shards) * per_item
     any_space = pl.BlockSpec(memory_space=pl.ANY)
     outs = pl.pallas_call(
         functools.partial(gather_kernel, ndp, nf, shapes),
@@ -159,17 +172,22 @@
         + [jax.ShapeDtypeStruct((nf,) + small.shape, small.dtype)],
         in_specs=[any_space] * (len(shards) + 1),
         out_specs=[any_space] * (len(shards) + 1),
-        scratch_shapes=[
+        scratch_shapes=[pltpu.VMEM(shape, jnp.bfloat16) for shape in shapes]
+        + [
             pltpu.SemaphoreType.DMA((copies,)),
             pltpu.SemaphoreType.DMA((copies,)),
             pltpu.SemaphoreType.DMA((len(shards) + 1,)),
         ],
-        compiler_params=pltpu.CompilerParams(collective_id=collective_id, has_side_effects=True),
+        compiler_params=pltpu.CompilerParams(
+            collective_id=collective_id, has_side_effects=True, vmem_limit_bytes=32 * 1024 * 1024
+        ),
         name="gather_weights",
     )(*shards, small)
     return outs[:-1], outs[-1]
 
 
+LAG = 2
+ROWS = 512
 def cut_plan(rows, cols, bits):
     plan = []
     for _ in range(bits):
@@ -311,10 +329,9 @@
 
     stores = []
     stages = fbits + 2 * dbits + 1
-    ahead = 2
-    for step in range(-ahead, len(chunks) + stages - 1):
+    for step in range(len(chunks) + LAG * (stages - 1)):
         for s in range(stages - 1, -1, -1):
-            j = step - s if s else step + ahead
+            j = step - LAG * s
             if 0 <= j < len(chunks):
                 stage(j, s)
     for copy, seen in started:
@@ -333,10 +350,10 @@
     shapes = tuple(g.shape for g in grads)
     fbits, dbits = log2(nf), log2(ndp)
     chunks = tuple(
-        (i, r0, c0, min(128, r // nf), min(1024, c))
+        (i, r0, c0, min(ROWS // nf, r // nf), min(1024, c))
         for i, (r, c) in enumerate(shapes)
         for c0 in range(0, c, min(1024, c))
-        for r0 in range(0, r // nf, min(128, r // nf))
+        for r0 in range(0, r // nf, min(ROWS // nf, r // nf))
     )
     n, half = len(chunks), nf // 2
     rn, cn = max(c[3] for c in chunks), max(c[4] for c in chunks)
@@ -372,6 +389,88 @@
     )(*grads)
 
 
+def nt(left, right):
+    return lax.dot_general(left, right, (((1,), (1,)), ((), ())), preferred_element_type=F32)
+
+
+def nn(left, right):
+    return jnp.dot(left, right, preferred_element_type=F32)
+
+
+def attend_kernel(q_ref, k_ref, v_ref, o_ref, probs_ref):
+    q, k, v = q_ref[...], k_ref[...], v_ref[...]
+    dim = q.shape[1] // 2
+    first = lax.broadcasted_iota(jnp.int32, q.shape, 1) < dim
+    parts = []
+    for h in range(2):
+        one = jnp.where(first if h == 0 else ~first, q, jnp.zeros_like(q))
+        scores = nt(one, k)
+        powers = jnp.exp(scores - jnp.max(scores, axis=1, keepdims=True))
+        probs = (powers * (1.0 / jnp.sum(powers, axis=1, keepdims=True))).astype(BF)
+        probs_ref[h] = probs
+        parts.append(nn(probs, v))
+    o_ref[...] = jnp.where(first, parts[0], parts[1]).astype(BF)
+
+
+def attention(q, k, v):
+    length, width = q.shape
+    pair = 2 * (width // HEADS)
+    cols = pl.BlockSpec((length, pair), lambda p: (0, p))
+    return pl.pallas_call(
+        attend_kernel,
+        grid=(HEADS // 2,),
+        in_specs=[cols] * 3,
+        out_specs=[cols, pl.BlockSpec((2, length, length), lambda p: (p, 0, 0))],
+        out_shape=[
+            jax.ShapeDtypeStruct((length, width), BF),
+            jax.ShapeDtypeStruct((HEADS, length, length), BF),
+        ],
+        compiler_params=pltpu.CompilerParams(vmem_limit_bytes=40 * 1024 * 1024),
+        name="attend",
+    )(q, k, v)
+
+
+def attend_back_math(q, k, v, o, do, probs, scale):
+    dim = q.shape[1] // 2
+    first = lax.broadcasted_iota(jnp.int32, q.shape, 1) < dim
+    product = do.astype(F32) * o.astype(F32)
+    q_t, do_t = q.T, do.T
+    dqs, dks, dvs = [], [], []
+    for h in range(2):
+        mine = first if h == 0 else ~first
+        inner = jnp.sum(jnp.where(mine, product, 0.0), axis=1, keepdims=True)
+        p = probs(h)
+        d_probs = nt(jnp.where(mine, do, jnp.zeros_like(do)), v)
+        d_scores = (p.astype(F32) * (d_probs - inner)).astype(BF)
+        dqs.append(nn(d_scores, k))
+        dks.append(nn(q_t[h * dim : (h + 1) * dim], d_scores))
+        dvs.append(nn(do_t[h * dim : (h + 1) * dim], p))
+    dq = jnp.where(first, dqs[0], dqs[1]).astype(BF) * BF(scale)
+    return dq, jnp.concatenate(dks, axis=0).T.astype(BF), jnp.concatenate(dvs, axis=0).T.astype(BF)
+
+
+def attend_back_kernel(scale, q_ref, k_ref, v_ref, o_ref, do_ref, probs_ref, dq_ref, dk_ref, dv_ref):
+    dq_ref[...], dk_ref[...], dv_ref[...] = attend_back_math(
+        q_ref[...], k_ref[...], v_ref[...], o_ref[...], do_ref[...], lambda h: probs_ref[h], scale
+    )
+
+
+def attention_back(q, k, v, o, do, probs):
+    length, width = q.shape
+    pair = 2 * (width // HEADS)
+    scale = 1.0 / math.sqrt(width // HEADS)
+    cols = pl.BlockSpec((length, pair), lambda p: (0, p))
+    return pl.pallas_call(
+        functools.partial(attend_back_kernel, scale),
+        grid=(HEADS // 2,),
+        in_specs=[cols] * 5 + [pl.BlockSpec((2, length, length), lambda p: (p, 0, 0))],
+        out_specs=[cols] * 3,
+        out_shape=[jax.ShapeDtypeStruct((length, width), BF)] * 3,
+        compiler_params=pltpu.CompilerParams(vmem_limit_bytes=40 * 1024 * 1024),
+        name="attend_back",
+    )(q, k, v, o, do, probs)
+
+
 def dot(left, right):
     return jnp.dot(left, right, preferred_element_type=F32)
 
@@ -400,27 +499,6 @@
     m1 = jnp.mean(gg, axis=-1, keepdims=True)
     m2 = jnp.mean(gg * unit, axis=-1, keepdims=True)
     return (gg - m1 - unit * m2) * inverse, d_gain, d_shift
-
-
-def attention(q, k, v, length):
-    heads = lambda t: t.reshape(length, HEADS, -1)
-    scores = jnp.einsum("qhe,khe->hqk", heads(q), heads(k), preferred_element_type=F32)
-    probs = jax.nn.softmax(scores, axis=-1).astype(BF)
-    mixed = jnp.einsum("hqk,khe->qhe", probs, heads(v), preferred_element_type=F32)
-    return mixed.reshape(length, -1).astype(BF), probs
-
-
-def attention_back(q, k, v, probs, mixed, d_mixed, length):
-    heads = lambda t: t.reshape(length, HEADS, -1)
-    qh, kh, vh, doh = heads(q), heads(k), heads(v), heads(d_mixed)
-    d_probs = jnp.einsum("qhe,khe->hqk", doh, vh, preferred_element_type=F32)
-    inner = jnp.einsum("qhe,qhe->hq", doh.astype(F32), heads(mixed).astype(F32))[:, :, None]
-    d_scores = (probs.astype(F32) * (d_probs - inner)).astype(BF)
-    dq = jnp.einsum("hqk,khe->qhe", d_scores, kh, preferred_element_type=F32).astype(BF)
-    dk = jnp.einsum("hqk,qhe->khe", d_scores, qh, preferred_element_type=F32).astype(BF)
-    dv = jnp.einsum("hqk,qhe->khe", probs, doh, preferred_element_type=F32).astype(BF)
-    flat = lambda t: t.reshape(length, -1)
-    return flat(dq), flat(dk), flat(dv)
 
 
 def forward(rows, w, length):
@@ -431,7 +509,7 @@
     q = ((joined[:, :width] + w["b_qv"][:width]) * scale).astype(BF)
     k = joined[:, width : 2 * width].astype(BF)
     v = (joined[:, 2 * width :] + w["b_qv"][width:]).astype(BF)
-    mixed, probs = attention(q, k, v, length)
+    mixed, probs = attention(q, k, v)
     branch = dot(mixed, w["out"]) + w["b_out"]
     hidden, unit1, inv1 = norm_forward(rows + branch, w["gain1"], w["bias1"])
     hidden_low = hidden.astype(BF)
@@ -458,8 +536,7 @@
     d_xz, d_gain1, d_bias1 = norm_back(gh, kept["unit1"], kept["inv1"], w["gain1"])
     dz = d_xz.astype(BF)
     d_mixed = back_dot(dz, w["out"]).astype(BF)
-    dq, dk, dv = attention_back(kept["q"], kept["k"], kept["v"], kept["probs"], kept["mixed"], d_mixed, length)
-    dq = dq * BF(scale)
+    dq, dk, dv = attention_back(kept["q"], kept["k"], kept["v"], kept["mixed"], d_mixed, kept["probs"])
     d_joined = jnp.concatenate([dq, dk, dv], axis=1)
     d_rows = d_xz + back_dot(d_joined, w["qkv"])
     vectors = (
@@ -506,8 +583,6 @@
         both = lambda a, b: jnp.concatenate([a, b], axis=0)
         return outer_dot(both(kept_one[left], kept_two[left]), both(one[right], two[right])).astype(BF)
 
-    (g_down,) = reduce_grads(ndp, nf, 1, [weight("active", "df")])
-    (g_up,) = reduce_grads(ndp, nf, 2, [weight("hidden", "du")])
     high = d_start.astype(BF)
     rest = d_start - high.astype(F32)
     mid = rest.astype(BF)
@@ -519,7 +594,9 @@
     vec_rows = 64 - table_rows
     pieces = jnp.pad(pieces, ((0, 0), (0, vec_rows * width - count))).astype(BF).reshape(nf, vec_rows, width)
     extra = jnp.concatenate([pieces, jnp.broadcast_to(d_table[None], (nf,) + d_table.shape)], axis=1).reshape(-1, width)
-    g_out, g_qkv, g_extra = reduce_grads(ndp, nf, 3, [weight("mixed", "dz"), weight("low", "d_joined"), extra])
+    g_down, g_up, g_out, g_qkv, g_extra = reduce_grads(
+        ndp, nf, 1, [weight("active", "df"), weight("hidden", "du"), weight("mixed", "dz"), weight("low", "d_joined"), extra]
+    )
     table_grad = g_extra[vec_rows : vec_rows + replace_table.shape[0]].astype(F32)
     flat = g_extra[:vec_rows].reshape(-1).astype(F32)
     v = []

time: 765 us -> 509 us (0.67)
  Pallas kernels: 457 us -> 300 us
  matrix products: 214 us -> 146 us
  other arithmetic: 48.4 us -> 30.1 us
  local copies, waits for them, and re-layouts: 33.6 us -> 22.6 us
    pallas_call x1, Pallas kernels: 197 us -> 68.4 us  [gather_weights(): pl.pallas_call(functools.partial(gather_kernel, ndp, nf, shapes), out_sha...]
    pallas_call x3 -> x1, Pallas kernels: 261 us -> 182 us  [reduce_grads(): pl.pallas_call(functools.partial(reduce_kernel, ndp, nf, shapes, chunks),...]
    pallas_call x0 -> x4, Pallas kernels: none -> 49.3 us  [the longest x2 26.7 us: attention_back(): pl.pallas_call(functools.partial(attend_back_kernel, scale), grid=(HEADS...]
    dot_general x10 -> x0, matrix products: 37.6 us -> none  [the longest x2 14.2 us: attention_back(): jnp.einsum('hqk,qhe->khe', probs, doh, preferred_element_type=F32)]
    sub x2 -> x0, matrix products: 18.3 us -> none  [attention(): probs = jax.nn.softmax(scores, axis=-1).astype(BF)]
    convert_element_type x4 -> x2, other arithmetic: 17.7 us -> 1.23 us  [forward(): v = (joined[:, 2 * width:] + w['b_qv'][width:]).astype(BF)]
    dot_general x7, matrix products: 48.7 us -> 37.9 us  [outer_dot(): lax.dot_general(left, right, (((0,), (0,)), ((), ())), preferred_element_...]
    convert_element_type x6 -> x0, local copies, waits for them, and re-layouts: 9.31 us -> none  [the longest x2 3.37 us: forward(): v = (joined[:, 2 * width:] + w['b_qv'][width:]).astype(BF)]
where the time goes in v2:
time: 509 us; the launch traced here: 501 us
  Pallas kernels  300 us (59%)
  matrix products  146 us (29%)
  other arithmetic  30.1 us (6%)
  local copies, waits for them, and re-layouts  22.6 us (4%)
    pallas_call x1, Pallas kernels, reduce_grads(): pl.pallas_call(functools.partial(reduce_kernel, ndp, nf, shapes, chunks),...  182 us
    pallas_call x1, Pallas kernels, gather_weights(): pl.pallas_call(functools.partial(gather_kernel, ndp, nf, shapes), out_sha...  68.4 us
    dot_general x8, matrix products, back_dot(): lax.dot_general(left, right, (((1,), (1,)), ((), ())), preferred_element_...  65.9 us
    dot_general x9, matrix products, dot(): return jnp.dot(left, right, preferred_element_type=F32)  42.2 us
    dot_general x7, matrix products, outer_dot(): lax.dot_general(left, right, (((0,), (0,)), ((), ())), preferred_element_...  37.9 us
    pallas_call x2, Pallas kernels, attention_back(): pl.pallas_call(functools.partial(attend_back_kernel, scale), grid=(HEADS...  26.7 us
    pallas_call x2, Pallas kernels, attention(): pl.pallas_call(attend_kernel, grid=(HEADS // 2,), in_specs=[cols] * 3, ou...  22.6 us
    unnamed x150, local copies, waits for them, and re-layouts  19.3 us

profile of v2, /device:TPU:0, one launch (start us, length us, event | category | flops | bytes accessed | tf_op | source)
XLA Modules:
  0.0 501.2 jit_solution(12796494812760715946)
XLA Ops:
  9.8 1.8 fusion.85
  14.8 68.4 %gather_weights.1 = (bf16[1024,3072]{1,0:T(8,128)(2,1)S(1)}, bf16[1024,1024]{1,0:T(8,128)(2,1)S(1)}, bf16[1024,4096]{1,0:T(8,128)(2,1)}, bf16[4096,1024]{1,0:T(8,128)(2,1)}, bf16[4,16,256]{2,1,0:T(8,128)(2,1)S(1)}) custom-call(bf16[256,3072]{1,0:T(8,128)(2,1)S(1)} %copy-done.12, bf16[256,1024]{1,0:T(8,128)(2,1)S(1)} %copy-done.17, ...), custom_call_target="tpu_custom_call" | custom-call | tf_op jit(solution)/shard_map/gather_weights/pallas_call | solution.py:169
  83.4 3.4 fusion.90
  88.1 11.2 %attend.2 = (bf16[512,1024]{1,0:T(8,128)(2,1)S(1)}, bf16[16,512,512]{2,1,0:T(8,128)(2,1)S(1)}) custom-call(bf16[512,1024]{1,0:T(8,128)(2,1)S(1)} %get-tuple-element.85.q_ref, bf16[512,1024]{1,0:T(8,128)(2,1)S(1)} %slice.171.k_ref, bf16[512,1024]{1,0:T(8,128)(2,1)S(1)} %get-tuple-element.84.v_ref), custom_call_target="tpu_custom_call" | custom-call | tf_op jit(solution)/shard_map/attend/pallas_call | solution.py:419
  100.7 1.8 copy-done.8
  103.7 10.9 %multiply_convert_fusion.3 = (bf16[512,4096]{1,0:T(8,128)(2,1)S(1)}, f32[512,4096]{1,0:T(8,128)}) fusion(f32[4096]{0:T(1024)S(1)} %bitcast.115, bf16[512,1024]{1,0:T(8,128)(2,1)S(1)} %fusion.65, bf16[1024,4096]{1,0:T(8,128)(2,1)} %get-tuple-element.39), kind=kOutput, calls=%fused_computation.26 | convolution fusion | flops 4307550208 | bytes 22036480 | tf_op jit(solution)/shard_map/dot_general | solution.py:475
  114.6 4.8 fusion.87
  120.2 3.4 fusion.91
  124.5 11.4 %attend.3 = (bf16[512,1024]{1,0:T(8,128)(2,1)S(1)}, bf16[16,512,512]{2,1,0:T(8,128)(2,1)S(1)}) custom-call(bf16[512,1024]{1,0:T(8,128)(2,1)S(1)} %get-tuple-element.83.q_ref, bf16[512,1024]{1,0:T(8,128)(2,1)S(1)} %slice.170.k_ref, bf16[512,1024]{1,0:T(8,128)(2,1)S(1)} %get-tuple-element.82.v_ref), custom_call_target="tpu_custom_call" | custom-call | tf_op jit(solution)/shard_map/attend/pallas_call | solution.py:419
  139.9 10.2 %multiply_convert_fusion.2 = (bf16[512,4096]{1,0:T(8,128)(2,1)S(1)}, f32[512,4096]{1,0:T(8,128)}) fusion(f32[4096]{0:T(1024)S(1)} %bitcast.116, bf16[512,1024]{1,0:T(8,128)(2,1)S(1)} %fusion.67, bf16[1024,4096]{1,0:T(8,128)(2,1)} %get-tuple-element.39), kind=kOutput, calls=%fused_computation.24 | convolution fusion | flops 4307550208 | bytes 22036480 | tf_op jit(solution)/shard_map/dot_general | solution.py:475
  150.1 4.8 fusion.89
  157.1 1.9 convert_reduce_fusion.3
  159.0 12.4 %convert_reduce_fusion = (f32[4096]{0:T(1024)S(1)}, bf16[512,4096]{1,0:T(8,128)(2,1)}) fusion(f32[512,4096]{1,0:T(8,128)} %get-tuple-element.112, f32[4096]{0:T(1024)S(1)} %bitcast.117, bf16[512,1024]{1,0:T(8,128)(2,1)S(1)} %get-tuple-element.72, bf16[4096,1024]{1,0:T(8,128)(2,1)} %get-tuple-element.40), kind=kOutput, calls=%fused_computation.20 | convolution fusion | flops 4326420480 | bytes 22052864 | tf_op jit(solution)/shard_map/dot_general | solution.py:479
  171.4 10.2 %multiply_reduce_fusion.1 = (f32[1024]{0:T(1024)S(1)}, f32[512]{0:T(512)S(1)}, f32[512]{0:T(512)S(1)}, f32[1024]{0:T(1024)S(1)}, f32[512,1024]{1,0:T(8,128)S(1)}) fusion(f32[512,1024]{1,0:T(8,128)S(1)} %get-tuple-element.110, f32[512]{0:T(512)S(1)} %add_rsqrt_fusion.1, f32[512]{0:T(512)S(1)} %broadcast_multiply_fusion.10, f32[1024]{0:T(1024)S(1)} %bitcast.90, ...), kind=kOutput, calls=%fused_computation.77 | convolution fusion | flops 4304401408 | bytes 19955712 | tf_op jit(solution)/shard_map/dot_general | solution.py:479
  181.6 2.0 convert_reduce_fusion.5
  185.0 13.4 %attend_back.2 = (bf16[512,1024]{1,0:T(8,128)(2,1)S(1)}, bf16[512,1024]{1,0:T(8,128)(2,1)S(1)}, bf16[512,1024]{1,0:T(8,128)(2,1)S(1)}) custom-call(bf16[512,1024]{1,0:T(8,128)(2,1)S(1)} %get-tuple-element.83.q_ref, bf16[512,1024]{1,0:T(8,128)(2,1)S(1)} %slice.170.k_ref, bf16[512,1024]{1,0:T(8,128)(2,1)S(1)} %get-tuple-element.82.v_ref, ...), custom_call_target="tpu_custom_call" | custom-call | tf_op jit(solution)/shard_map/attend_back/pallas_call | solution.py:463
  201.0 9.2 %multiply_reduce_fusion = (f32[1024]{0:T(1024)S(1)}, f32[512]{0:T(512)S(1)}, f32[512]{0:T(512)S(1)}, f32[1024]{0:T(1024)S(1)}, f32[512,1024]{1,0:T(8,128)}) fusion(f32[512,1024]{1,0:T(8,128)S(1)} %copy-done.24, f32[512]{0:T(512)S(1)} %add_rsqrt_fusion.2, f32[512]{0:T(512)S(1)} %broadcast_multiply_fusion.11, f32[1024]{0:T(1024)S(1)} %bitcast.99, ...), kind=kOutput, calls=%fused_computation.74 | convolution fusion | flops 3226465280 | bytes 15749120 | tf_op jit(solution)/shard_map/dot_general | solution.py:479
  210.3 3.6 convert_reduce_fusion.4
  213.9 12.1 %convert_reduce_fusion.1 = (f32[4096]{0:T(1024)S(1)}, bf16[512,4096]{1,0:T(8,128)(2,1)}) fusion(f32[512,4096]{1,0:T(8,128)} %get-tuple-element.106, f32[4096]{0:T(1024)S(1)} %bitcast.118, bf16[512,1024]{1,0:T(8,128)(2,1)S(1)} %get-tuple-element.74, bf16[4096,1024]{1,0:T(8,128)(2,1)} %get-tuple-element.40), kind=kOutput, calls=%fused_computation.21 | convolution fusion | flops 4326420480 | bytes 22052864 | tf_op jit(solution)/shard_map/dot_general | solution.py:479
  226.1 12.5 %fusion.21.refs_0_ = bf16[4096,1024]{1,0:T(8,128)(2,1)} fusion(bf16[512,4096]{1,0:T(8,128)(2,1)S(1)} %copy-done.53, bf16[512,4096]{1,0:T(8,128)(2,1)S(1)} %copy-done.51, bf16[512,1024]{1,0:T(8,128)(2,1)S(1)} %copy-done.43, bf16[512,1024]{1,0:T(8,128)(2,1)S(1)} %get-tuple-element.74), kind=kOutput, calls=%fused_computation.29 | convolution fusion | flops 8615100416 | bytes 18874368 | tf_op jit(solution)/shard_map/dot_general | solution.py:483
  238.7 11.6 %multiply_reduce_fusion.2 = (f32[1024]{0:T(1024)S(1)}, f32[512]{0:T(512)S(1)}, f32[512]{0:T(512)S(1)}, f32[1024]{0:T(1024)S(1)}, f32[512,1024]{1,0:T(8,128)}) fusion(f32[512,1024]{1,0:T(8,128)S(1)} %copy-done.22, f32[512]{0:T(512)S(1)} %add_rsqrt_fusion.3, f32[512]{0:T(512)S(1)} %broadcast_multiply_fusion.12, f32[1024]{0:T(1024)S(1)} %bitcast.92, ...), kind=kOutput, calls=%fused_computation.78 | convolution fusion | flops 4300207104 | bytes 18894848 | tf_op jit(solution)/shard_map/dot_general | solution.py:479
  250.3 11.1 %fusion.18.refs_1_ = bf16[1024,4096]{1,0:T(8,128)(2,1)} fusion(bf16[512,4096]{1,0:T(8,128)(2,1)S(1)} %copy-done.55, bf16[512,4096]{1,0:T(8,128)(2,1)S(1)} %copy-done.54, bf16[512,1024]{1,0:T(8,128)(2,1)S(1)} %copy-done.39, bf16[512,1024]{1,0:T(8,128)(2,1)S(1)} %copy-done.37), kind=kOutput, calls=%fused_computation.28 | convolution fusion | flops 8615100416 | bytes 18874368 | tf_op jit(solution)/shard_map/dot_general | solution.py:483
  261.5 3.7 convert_reduce_fusion.6
  267.4 13.3 %attend_back.3 = (bf16[512,1024]{1,0:T(8,128)(2,1)S(1)}, bf16[512,1024]{1,0:T(8,128)(2,1)S(1)}, bf16[512,1024]{1,0:T(8,128)(2,1)S(1)}) custom-call(bf16[512,1024]{1,0:T(8,128)(2,1)S(1)} %copy-done.7, bf16[512,1024]{1,0:T(8,128)(2,1)S(1)} %copy-done.3, bf16[512,1024]{1,0:T(8,128)(2,1)S(1)} %copy-done.5, bf16[512,1024]{1,0:T(8,128)(2,1)S(1)} %copy-done.14, ...), custom_call_target="tpu_custom_call" | custom-call | tf_op jit(solution)/shard_map/attend_back/pallas_call | solution.py:463
  280.7 3.7 fusion.60.refs_2_
  286.8 7.7 %broadcast_multiply_fusion = (f32[512,1024]{1,0:T(8,128)}, f32[512,1024]{1,0:T(8,128)S(1)}) fusion(f32[512]{0:T(512)S(1)} %copy-done.49, f32[512,1024]{1,0:T(8,128)S(1)} %copy-done.27, bf16[512,3072]{1,0:T(8,128)(2,1)S(1)} %constant_dynamic-update-slice_fusion.3, bf16[1024,3072]{1,0:T(8,128)(2,1)} %copy-done.18), kind=kOutput, calls=%fused_computation.124 | convolution fusion | flops 3222274048 | bytes 15730688 | tf_op jit(solution)/shard_map/dot_general | solution.py:479
  294.5 9.1 %fusion.28.refs_3_ = bf16[1024,3072]{1,0:T(8,128)(2,1)} fusion(bf16[512,3072]{1,0:T(8,128)(2,1)S(1)} %copy-done.45, bf16[512,3072]{1,0:T(8,128)(2,1)S(1)} %constant_dynamic-update-slice_fusion.3, bf16[512,1024]{1,0:T(8,128)(2,1)S(1)} %copy-done.35, bf16[512,1024]{1,0:T(8,128)(2,1)S(1)} %copy-done.41), kind=kOutput, calls=%fused_computation.34 | convolution fusion | flops 6462373888 | bytes 14680064 | tf_op jit(solution)/shard_map/dot_general | solution.py:483
  305.1 182.0 %reduce_grads.1 = (bf16[1024,1024]{1,0:T(8,128)(2,1)}, bf16[256,4096]{1,0:T(8,128)(2,1)}, bf16[256,1024]{1,0:T(8,128)(2,1)}, bf16[256,3072]{1,0:T(8,128)(2,1)}, bf16[64,1024]{1,0:T(8,128)(2,1)}) custom-call(bf16[4096,1024]{1,0:T(8,128)(2,1)} %fusion.21.refs_0_, bf16[1024,4096]{1,0:T(8,128)(2,1)} %fusion.18.refs_1_, bf16[1024,1024]{1,0:T(8,128)(2,1)} %fusion.60.refs_2_, ...), custom_call_target="tpu_custom_call" | custom-call | tf_op jit(solution)/shard_map/reduce_grads/pallas_call | solution.py:367
  491.5 2.1 convert_element_type.310
  493.6 2.0 convert_element_type.307
  495.8 2.5 convert_element_type.311
  498.3 2.5 convert_element_type.312
  (227 shorter events, 37.5 us)
Async XLA Ops:
  0.6 9.2 %copy-start = (bf16[30,1024]{1,0:T(8,128)(2,1)S(1)}, bf16[30,1024]{1,0:T(8,128)(2,1)}, u32[]{:S(2)}) copy-start(bf16[30,1024]{1,0:T(8,128)(2,1)} %param.23) | copy-start | bytes 184324
  2.1 9.6 %copy-start.48 = (f32[512]{0:T(512)}, f32[512]{0:T(512)S(1)}, u32[]{:S(2)}) copy-start(f32[512]{0:T(512)S(1)} %broadcast_subtract_fusion) | copy-start | bytes 6148
  11.7 71.7 %copy-start.40 = (bf16[512,1024]{1,0:T(8,128)(2,1)}, bf16[512,1024]{1,0:T(8,128)(2,1)S(1)}, u32[]{:S(2)}) copy-start(bf16[512,1024]{1,0:T(8,128)(2,1)S(1)} %get-tuple-element.101) | copy-start | bytes 3145732
  83.2 37.0 %copy-start.18 = (bf16[1024,3072]{1,0:T(8,128)(2,1)}, bf16[1024,3072]{1,0:T(8,128)(2,1)S(1)}, u32[]{:S(2)}) copy-start(bf16[1024,3072]{1,0:T(8,128)(2,1)S(1)} %get-tuple-element.35) | copy-start | bytes 18874372
  83.2 100.4 %copy-start.19 = (bf16[1024,1024]{1,0:T(8,128)(2,1)}, bf16[1024,1024]{1,0:T(8,128)(2,1)S(1)}, u32[]{:S(2)}) copy-start(bf16[1024,1024]{1,0:T(8,128)(2,1)S(1)} %get-tuple-element.38) | copy-start | bytes 6291460
  87.7 13.0 %copy-start.4 = (bf16[512,1024]{1,0:T(8,128)(2,1)}, bf16[512,1024]{1,0:T(8,128)(2,1)S(1)}, u32[]{:S(2)}) copy-start(bf16[512,1024]{1,0:T(8,128)(2,1)S(1)} %get-tuple-element.84.v_ref) | copy-start | bytes 3145732
  87.7 13.0 %copy-start.6 = (bf16[512,1024]{1,0:T(8,128)(2,1)}, bf16[512,1024]{1,0:T(8,128)(2,1)S(1)}, u32[]{:S(2)}) copy-start(bf16[512,1024]{1,0:T(8,128)(2,1)S(1)} %get-tuple-element.85.q_ref) | copy-start | bytes 3145732
  102.9 11.7 %copy-start.21 = (f32[512,1024]{1,0:T(8,128)}, f32[512,1024]{1,0:T(8,128)S(1)}, u32[]{:S(2)}) copy-start(f32[512,1024]{1,0:T(8,128)S(1)} %get-tuple-element.104) | copy-start | bytes 6291460
  103.3 11.3 %slice-start = ((s8[8388608]{0:T(1024)(128)(4,1)}), s8[4194304]{0:T(1024)(128)(4,1)S(1)}, s32[]{:S(2)}) async-start(s8[8388608]{0:T(1024)(128)(4,1)} %bitcast.125), calls=%async_computation | async-start | bytes 8388608
  103.7 10.9 %copy-start.36 = (bf16[512,1024]{1,0:T(8,128)(2,1)}, bf16[512,1024]{1,0:T(8,128)(2,1)S(1)}, u32[]{:S(2)}) copy-start(bf16[512,1024]{1,0:T(8,128)(2,1)S(1)} %fusion.65) | copy-start | bytes 3145732
  103.7 10.9 %slice-start.1 = ((s8[8388608]{0:T(1024)(128)(4,1)}), s8[4194304]{0:T(1024)(128)(4,1)S(1)}, s32[]{:S(2)}) async-start(s8[8388608]{0:T(1024)(128)(4,1)} %bitcast.125), calls=%async_computation.1 | async-start | bytes 8388608
  119.4 16.5 %copy-start.23 = (f32[512,1024]{1,0:T(8,128)}, f32[512,1024]{1,0:T(8,128)S(1)}, u32[]{:S(2)}) copy-start(f32[512,1024]{1,0:T(8,128)S(1)} %get-tuple-element.108) | copy-start | bytes 6291460
  135.9 49.1 %copy-start.15 = (bf16[512,1024]{1,0:T(8,128)(2,1)}, bf16[512,1024]{1,0:T(8,128)(2,1)S(1)}, u32[]{:S(2)}) copy-start(bf16[512,1024]{1,0:T(8,128)(2,1)S(1)} %get-tuple-element.41.o_ref) | copy-start | bytes 3145732
  139.4 10.6 %slice-start.2 = ((s8[8388608]{0:T(1024)(128)(4,1)}), s8[4194304]{0:T(1024)(128)(4,1)S(1)}, s32[]{:S(2)}) async-start(s8[8388608]{0:T(1024)(128)(4,1)} %bitcast.127), calls=%async_computation.2 | async-start | bytes 8388608
  139.8 10.2 %copy-start.38 = (bf16[512,1024]{1,0:T(8,128)(2,1)}, bf16[512,1024]{1,0:T(8,128)(2,1)S(1)}, u32[]{:S(2)}) copy-start(bf16[512,1024]{1,0:T(8,128)(2,1)S(1)} %fusion.67) | copy-start | bytes 3145732
  139.9 10.2 %slice-start.3 = ((s8[8388608]{0:T(1024)(128)(4,1)}), s8[4194304]{0:T(1024)(128)(4,1)S(1)}, s32[]{:S(2)}) async-start(s8[8388608]{0:T(1024)(128)(4,1)} %bitcast.127), calls=%async_computation.3 | async-start | bytes 8388608
  159.0 12.4 %copy-start.42 = (bf16[512,1024]{1,0:T(8,128)(2,1)}, bf16[512,1024]{1,0:T(8,128)(2,1)S(1)}, u32[]{:S(2)}) copy-start(bf16[512,1024]{1,0:T(8,128)(2,1)S(1)} %get-tuple-element.72) | copy-start | bytes 3145732
  201.0 9.3 %copy-start.44 = (bf16[512,3072]{1,0:T(8,128)(2,1)}, bf16[512,3072]{1,0:T(8,128)(2,1)S(1)}, u32[]{:S(2)}) copy-start(bf16[512,3072]{1,0:T(8,128)(2,1)S(1)} %constant_dynamic-update-slice_fusion) | copy-start | bytes 9437188
  201.0 9.3 %copy-start.25 = (f32[512,1024]{1,0:T(8,128)S(1)}, f32[512,1024]{1,0:T(8,128)}, u32[]{:S(2)}) copy-start(f32[512,1024]{1,0:T(8,128)} %copy-done.23) | copy-start | bytes 6291460
  213.9 12.1 %copy-start.43 = (bf16[512,1024]{1,0:T(8,128)(2,1)S(1)}, bf16[512,1024]{1,0:T(8,128)(2,1)}, u32[]{:S(2)}) copy-start(bf16[512,1024]{1,0:T(8,128)(2,1)} %copy-done.42) | copy-start | bytes 3145732
  213.9 12.1 %copy-start.51 = (bf16[512,4096]{1,0:T(8,128)(2,1)S(1)}, bf16[512,4096]{1,0:T(8,128)(2,1)}, u32[]{:S(2)}) copy-start(bf16[512,4096]{1,0:T(8,128)(2,1)} %copy-done.50) | copy-start | bytes 12582916
  213.9 12.1 %copy-start.53 = (bf16[512,4096]{1,0:T(8,128)(2,1)S(1)}, bf16[512,4096]{1,0:T(8,128)(2,1)}, u32[]{:S(2)}) copy-start(bf16[512,4096]{1,0:T(8,128)(2,1)} %copy-done.52) | copy-start | bytes 12582916
  226.1 12.5 %copy-start.22 = (f32[512,1024]{1,0:T(8,128)S(1)}, f32[512,1024]{1,0:T(8,128)}, u32[]{:S(2)}) copy-start(f32[512,1024]{1,0:T(8,128)} %copy-done.21) | copy-start | bytes 6291460
  238.6 11.7 %copy-start.37 = (bf16[512,1024]{1,0:T(8,128)(2,1)S(1)}, bf16[512,1024]{1,0:T(8,128)(2,1)}, u32[]{:S(2)}) copy-start(bf16[512,1024]{1,0:T(8,128)(2,1)} %copy-done.36) | copy-start | bytes 3145732
  238.6 11.7 %copy-start.39 = (bf16[512,1024]{1,0:T(8,128)(2,1)S(1)}, bf16[512,1024]{1,0:T(8,128)(2,1)}, u32[]{:S(2)}) copy-start(bf16[512,1024]{1,0:T(8,128)(2,1)} %copy-done.38) | copy-start | bytes 3145732
  238.6 11.7 %copy-start.54 = (bf16[512,4096]{1,0:T(8,128)(2,1)S(1)}, bf16[512,4096]{1,0:T(8,128)(2,1)}, u32[]{:S(2)}) copy-start(bf16[512,4096]{1,0:T(8,128)(2,1)} %get-tuple-element.121) | copy-start | bytes 12582916
  238.6 11.6 %copy-start.55 = (bf16[512,4096]{1,0:T(8,128)(2,1)S(1)}, bf16[512,4096]{1,0:T(8,128)(2,1)}, u32[]{:S(2)}) copy-start(bf16[512,4096]{1,0:T(8,128)(2,1)} %get-tuple-element.123) | copy-start | bytes 12582916
  267.4 13.3 %copy-start.16 = (bf16[512,1024]{1,0:T(8,128)(2,1)S(1)}, bf16[512,1024]{1,0:T(8,128)(2,1)}, u32[]{:S(2)}) copy-start(bf16[512,1024]{1,0:T(8,128)(2,1)} %copy-done.15) | copy-start | bytes 3145732
  267.4 13.3 %copy-start.33 = (bf16[512,1024]{1,0:T(8,128)(2,1)S(1)}, bf16[512,1024]{1,0:T(8,128)(2,1)}, u32[]{:S(2)}) copy-start(bf16[512,1024]{1,0:T(8,128)(2,1)} %copy-done.32) | copy-start | bytes 3145732
  286.8 7.7 %copy-start.41 = (bf16[512,1024]{1,0:T(8,128)(2,1)S(1)}, bf16[512,1024]{1,0:T(8,128)(2,1)}, u32[]{:S(2)}) copy-start(bf16[512,1024]{1,0:T(8,128)(2,1)} %copy-done.40) | copy-start | bytes 3145732
  286.8 7.7 %copy-start.45 = (bf16[512,3072]{1,0:T(8,128)(2,1)S(1)}, bf16[512,3072]{1,0:T(8,128)(2,1)}, u32[]{:S(2)}) copy-start(bf16[512,3072]{1,0:T(8,128)(2,1)} %copy-done.44) | copy-start | bytes 9437188
  294.5 9.1 %copy-start.47 = (bf16[512,30]{0,1:T(8,128)(2,1)S(1)}, bf16[512,30]{0,1:T(8,128)(2,1)}, u32[]{:S(2)}) copy-start(bf16[512,30]{0,1:T(8,128)(2,1)} %copy-done.46) | copy-start | bytes 92164
  (28 other events, 77.0 us)

commit v3 on v2

--- a/solution.py
+++ b/solution.py
@@ -188,205 +188,215 @@
 
 LAG = 2
 ROWS = 512
-def cut_plan(rows, cols, bits):
-    plan = []
-    for _ in range(bits):
-        if rows >= 32:
-            rows //= 2
-            plan.append((0, rows))
+
+
+LAG = 2
+CHUNK_ROWS = 512
+CORE_SLOTS = 4
+HELD_SLOTS = 14
+KINDS = (0,)
+
+
+def al(value, by):
+    return value if isinstance(value, int) else pl.multiple_of(value, by)
+
+
+def stage_orders(ndp, nf):
+    outer = [("outer", b) for b in range(log2(nf) - 1, 0, -1)]
+    near = [("near", b) for b in range(log2(ndp))]
+    return (
+        outer + near,
+        near[:1] + outer + near[1:],
+        outer + near[1:2] + near[:1] + near[2:],
+    )
+
+
+def chunk_list(ndp, nf, shapes, kinds):
+    chunks = []
+    for i, (r, c) in enumerate(shapes):
+        rn, cn = min(CHUNK_ROWS // nf, r // nf), min(1024, c)
+        for c0 in range(0, c, cn):
+            for r0 in range(0, r // nf, rn):
+                chunks.append((i, r0, c0, rn, cn, kinds[len(chunks) % len(kinds)]))
+    return tuple(chunks)
+
+
+def halvings(order, half, rn, cn):
+    left, blocks = [], half
+    for kind, _ in order:
+        if kind == "outer":
+            blocks //= 2
+            axis = 0
+        elif rn >= 32:
+            rn //= 2
+            axis = 1
         else:
-            cols //= 2
-            plan.append((1, cols))
-    return plan
-
-
-def reduce_kernel(ndp, nf, shapes, chunks, *refs):
-    n = len(shapes)
-    ins, outs = refs[:n], refs[n : 2 * n]
-    held, from_core = refs[2 * n : 2 * n + 2]
-    rest = refs[2 * n + 2 :]
-    fbits, dbits = log2(nf), log2(ndp)
-    from_outer, rest = rest[: fbits - 1], rest[fbits - 1 :]
-    from_near, rest = rest[:dbits], rest[dbits:]
-    done, send, recv, local, store = rest
-    dp, me = lax.axis_index("dp"), lax.axis_index("fsdp")
-    core = lax.rem(me, 2)
-    sibling = (dp, flip(me, 0))
-    outer = [(dp, flip(me, b)) for b in range(1, fbits)]
-    near = [(flip(dp, b), me) for b in range(dbits)]
-    entry_barrier([sibling] + outer + near)
-    half = nf // 2
-    started = []
-    state = {}
-
-    def push(src, dst, partner):
-        k = len(started)
+            cn //= 2
+            axis = 2
+        left.append((blocks, rn, cn, axis))
+    return left
+
+
+def engine_scratch(ndp, nf, chunks):
+    orders, half = stage_orders(ndp, nf), nf // 2
+    rn, cn = max(c[3] for c in chunks), max(c[4] for c in chunks)
+    scratch = [
+        pltpu.VMEM((HELD_SLOTS, half, rn, cn), jnp.bfloat16),
+        pltpu.VMEM((CORE_SLOTS, half, rn, cn), jnp.bfloat16),
+        pltpu.VMEM((len(chunks), rn, cn), jnp.bfloat16),
+    ]
+    for kind, order in enumerate(orders):
+        mine = [c for c in chunks if c[5] == kind]
+        if mine:
+            sizes = [halvings(order, half, c[3], c[4]) for c in mine]
+            for s in range(len(order)):
+                most = tuple(max(size[s][a] for size in sizes) for a in range(3))
+                scratch.append(pltpu.VMEM((2 * LAG,) + most, jnp.bfloat16))
+    copies = len(chunks) * (half + len(orders[0]) + log2(ndp))
+    return scratch + [
+        pltpu.SemaphoreType.DMA((copies,)),
+        pltpu.SemaphoreType.DMA((copies,)),
+        pltpu.SemaphoreType.DMA((len(chunks) * half,)),
+        pltpu.SemaphoreType.DMA((len(chunks),)),
+    ]
+
+
+class Engine:
+    def __init__(self, ndp, nf, chunks, refs, source, target):
+        self.nf, self.chunks, self.source, self.target = nf, chunks, source, target
+        self.orders, self.half = stage_orders(ndp, nf), nf // 2
+        self.dbits = log2(ndp)
+        self.held, self.from_core, self.done = refs[:3]
+        self.landing = {}
+        at = 3
+        for kind in range(len(self.orders)):
+            if any(c[5] == kind for c in chunks):
+                for s in range(len(self.orders[0])):
+                    self.landing[kind, s] = refs[at]
+                    at += 1
+        self.send, self.recv, self.local, self.store = refs[at:]
+        self.dp, self.me = lax.axis_index("dp"), lax.axis_index("fsdp")
+        self.core = lax.rem(self.me, 2)
+        self.sibling = (self.dp, flip(self.me, 0))
+        self.partner = {("outer", b): (self.dp, flip(self.me, b)) for b in range(1, log2(nf))}
+        self.partner.update({("near", b): (flip(self.dp, b), self.me) for b in range(self.dbits)})
+        self.started, self.state, self.stores, self.used = [], {}, [], {}
+        self.sends = {}
+        counts = {}
+        self.index = []
+        for c in chunks:
+            self.index.append(counts.get(c[5], 0) % (2 * LAG))
+            counts[c[5]] = counts.get(c[5], 0) + 1
+        self.stages = 2 + len(self.orders[0]) + self.dbits
+        self.steps = len(chunks) + LAG * (self.stages - 1)
+        entry_barrier([self.sibling] + list(self.partner.values()))
+
+    def push(self, src, dst, partner, holder=None):
+        k = len(self.started)
         copy = pltpu.make_async_remote_copy(
-            src, dst, send.at[k], recv.at[k], device_id=partner, device_id_type=MESH
+            src, dst, self.send.at[k], self.recv.at[k], device_id=partner, device_id_type=MESH
         )
         copy.start()
-        started.append([copy, False])
+        self.started.append([copy, False, False])
+        if holder is not None:
+            self.sends.setdefault(holder, []).append(k)
         return k
 
-    def arrive(k):
-        started[k][0].wait_recv()
-        started[k][1] = True
-
-    def window(j, block, at):
-        (r0, rr), (c0, cc) = at
-        return held.at[j, block, pl.ds(r0, rr), pl.ds(c0, cc)]
-
-    def stage(j, s):
-        i, r0, c0, rn, cn = chunks[j]
-        plan = cut_plan(rn, cn, dbits)
-        block_rows = shapes[i][0] // nf
+    def arrive(self, k):
+        self.started[k][0].wait_recv()
+        self.started[k][1] = True
+
+    def sent(self, holder):
+        for k in self.sends.pop(holder, []):
+            self.started[k][0].wait_send()
+            self.started[k][2] = True
+
+    def block_row(self, j, b, other):
+        i, r0 = self.chunks[j][:2]
+        core = 1 - self.core if other else self.core
+        return (2 * b + core, r0)
+
+    def slot(self, j):
+        return j % HELD_SLOTS
+
+    def room(self, j):
+        self.sent(("held", self.slot(j)))
+
+    def stage(self, j, s):
+        i, r0, c0, rn, cn, kind = self.chunks[j]
+        order = self.orders[kind]
+        held, slot = self.held, self.slot(j)
+        last = len(order)
         if s == 0:
-            loads, sends = [], []
-            for b in range(half):
-                mine = ins[i].at[pl.ds(pl.multiple_of((2 * b + core) * block_rows + r0, 16), rn), pl.ds(c0, cn)]
-                theirs = ins[i].at[pl.ds(pl.multiple_of((2 * b + 1 - core) * block_rows + r0, 16), rn), pl.ds(c0, cn)]
-                copy = pltpu.make_async_copy(mine, held.at[j, b, pl.ds(0, rn), pl.ds(0, cn)], local.at[j * half + b])
-                copy.start()
-                loads.append(copy)
-                sends.append(push(theirs, from_core.at[j, b, pl.ds(0, rn), pl.ds(0, cn)], sibling))
-            state[j] = (loads, sends)
+            self.room(j)
+            self.state[j] = self.source(self, j)
             return
         if s == 1:
-            loads, sends = state[j]
-            for b in range(half):
-                loads[b].wait()
-                arrive(sends[b])
-            held[j, :, :rn, :cn] += from_core[j, :, :rn, :cn]
-            state[j] = (0, half)
-        elif s < fbits + 1:
-            bit = fbits - (s - 1)
-            k, lo, size = state[j]
-            arrive(k)
-            held[j, pl.ds(lo, size), :rn, :cn] += from_outer[bit - 1][j, :, :rn, :cn]
-            state[j] = (lo, size)
-        if 1 <= s < fbits:
-            bit = fbits - s
-            lo, size = state[j]
+            loads, sends = self.state[j]
+            for copy in loads:
+                copy.wait()
+            for k in sends:
+                self.arrive(k)
+            held[slot, :, :rn, :cn] += self.from_core[j % CORE_SLOTS, :, :rn, :cn]
+            now, history = ((0, self.half), (0, rn), (0, cn)), []
+        elif s <= last + 1:
+            k, now, history = self.state[j]
+            self.arrive(k)
+            (b0, bn), (ra, rr), (ca, cc) = now
+            arrived = self.landing[kind, s - 2][self.index[j], :bn, :rr, :cc]
+            total = held[slot, pl.ds(b0, bn), pl.ds(ra, rr), pl.ds(ca, cc)] + arrived
+            if s == last + 1:
+                self.done[j, pl.ds(ra, rr), pl.ds(ca, cc)] = total[0]
+            else:
+                held[slot, pl.ds(b0, bn), pl.ds(ra, rr), pl.ds(ca, cc)] = total
+        if s <= last:
+            name, bit = order[s - 1]
+            axis = halvings(order, self.half, rn, cn)[s - 1][3]
+            mine = bit_of(self.me if name == "outer" else self.dp, bit)
+            start, size = now[axis]
             size //= 2
-            mine = bit_of(me, bit)
-            keep, give = lo + mine * size, lo + (1 - mine) * size
-            k = push(
-                held.at[j, pl.ds(give, size), pl.ds(0, rn), pl.ds(0, cn)],
-                from_outer[bit - 1].at[j, :, pl.ds(0, rn), pl.ds(0, cn)],
-                outer[bit - 1],
+            by = (1, 16, 128)[axis]
+            keep, give = list(now), list(now)
+            keep[axis] = (al(start + mine * size, by), size)
+            give[axis] = (al(start + (1 - mine) * size, by), size)
+            src = held.at[(slot,) + tuple(pl.ds(*g) for g in give)]
+            dst = self.landing[kind, s - 1].at[(self.index[j],) + tuple(pl.ds(0, g[1]) for g in give)]
+            k = self.push(src, dst, self.partner[name, bit], ("held", slot))
+            if name == "near":
+                history = history + [(bit, now[1:])]
+            self.state[j] = (k, tuple(keep), history)
+            return
+        if s > last + 1:
+            k, _, history = self.state[j]
+            self.arrive(k)
+            at, history = history[-1][1], history[:-1]
+        else:
+            at = now[1:]
+        if history:
+            piece = self.done.at[(j,) + tuple(pl.ds(*a) for a in at)]
+            k = self.push(piece, piece, self.partner["near", history[-1][0]])
+            self.state[j] = (k, None, history)
+        else:
+            copy = pltpu.make_async_copy(
+                self.done.at[j, pl.ds(0, rn), pl.ds(0, cn)], self.target(j), self.store.at[j]
             )
-            state[j] = (k, keep, size)
-            return
-        first = fbits
-        if first <= s <= first + dbits:
-            b = s - first
-            if b == 0:
-                lo, _ = state[j]
-                at = ((0, rn), (0, cn))
-            else:
-                k, lo, at, history = state[j]
-                arrive(k)
-                (ra, rr), (ca, cc) = at
-                total = held[j, lo, pl.ds(ra, rr), pl.ds(ca, cc)] + from_near[b - 1][j, :rr, :cc]
-                if b == dbits:
-                    done[j, pl.ds(ra, rr), pl.ds(ca, cc)] = total
-                else:
-                    held[j, lo, pl.ds(ra, rr), pl.ds(ca, cc)] = total
-            if b < dbits:
-                (ra, rr), (ca, cc) = at
-                axis, size = plan[b]
-                mine = bit_of(dp, b)
-                if axis == 0:
-                    keep = ((al(ra + mine * size, 16), size), (ca, cc))
-                    give = ((al(ra + (1 - mine) * size, 16), size), (ca, cc))
-                else:
-                    keep = ((ra, rr), (al(ca + mine * size, 128), size))
-                    give = ((ra, rr), (al(ca + (1 - mine) * size, 128), size))
-                k = push(
-                    window(j, lo, give), from_near[b].at[j, pl.ds(0, keep[0][1]), pl.ds(0, keep[1][1])], near[b]
-                )
-                history = [] if b == 0 else state[j][3]
-                state[j] = (k, lo, keep, history + [at])
-                return
-            _, _, at, history = state[j]
-        if s == first + dbits:
-            at, history = state[j][2], state[j][3]
-        else:
-            b = dbits - (s - first - dbits)
-            k, at, history = state[j]
-            arrive(k)
-            at, history = history[-1], history[:-1]
-        if history:
-            b = len(history) - 1
-            (ra, rr), (ca, cc) = at
-            piece = done.at[j, pl.ds(ra, rr), pl.ds(ca, cc)]
-            k = push(piece, piece, near[b])
-            state[j] = (k, at, history)
-        else:
-            copy = pltpu.make_async_copy(done.at[j, pl.ds(0, rn), pl.ds(0, cn)], outs[i].at[pl.ds(r0, rn), pl.ds(c0, cn)], store.at[j])
             copy.start()
-            stores.append(copy)
-
-    stores = []
-    stages = fbits + 2 * dbits + 1
-    for step in range(len(chunks) + LAG * (stages - 1)):
-        for s in range(stages - 1, -1, -1):
-            j = step - LAG * s
-            if 0 <= j < len(chunks):
-                stage(j, s)
-    for copy, seen in started:
-        copy.wait_send()
-        if not seen:
-            copy.wait_recv()
-    for copy in stores:
-        copy.wait()
-
-
-def al(value, by):
-    return value if isinstance(value, int) else pl.multiple_of(value, by)
-
-
-def reduce_grads(ndp, nf, collective_id, grads):
-    shapes = tuple(g.shape for g in grads)
-    fbits, dbits = log2(nf), log2(ndp)
-    chunks = tuple(
-        (i, r0, c0, min(ROWS // nf, r // nf), min(1024, c))
-        for i, (r, c) in enumerate(shapes)
-        for c0 in range(0, c, min(1024, c))
-        for r0 in range(0, r // nf, min(ROWS // nf, r // nf))
-    )
-    n, half = len(chunks), nf // 2
-    rn, cn = max(c[3] for c in chunks), max(c[4] for c in chunks)
-    sizes = [(0, 0)] * dbits
-    for _, _, _, rr, cc in chunks:
-        for b, (axis, size) in enumerate(cut_plan(rr, cc, dbits)):
-            rr, cc = (size, cc) if axis == 0 else (rr, size)
-            sizes[b] = max(sizes[b][0], rr), max(sizes[b][1], cc)
-    copies = n * (half + fbits - 1 + 2 * dbits)
-    any_space = pl.BlockSpec(memory_space=pl.ANY)
-    return pl.pallas_call(
-        functools.partial(reduce_kernel, ndp, nf, shapes, chunks),
-        out_shape=[jax.ShapeDtypeStruct((r // nf, c), jnp.bfloat16) for r, c in shapes],
-        in_specs=[any_space] * len(grads),
-        out_specs=[any_space] * len(grads),
-        scratch_shapes=[
-            pltpu.VMEM((n, half, rn, cn), jnp.bfloat16),
-            pltpu.VMEM((n, half, rn, cn), jnp.bfloat16),
-        ]
-        + [pltpu.VMEM((n, 1 << (b - 1), rn, cn), jnp.bfloat16) for b in range(1, fbits)]
-        + [pltpu.VMEM((n,) + size, jnp.bfloat16) for size in sizes]
-        + [
-            pltpu.VMEM((n, rn, cn), jnp.bfloat16),
-            pltpu.SemaphoreType.DMA((copies,)),
-            pltpu.SemaphoreType.DMA((copies,)),
-            pltpu.SemaphoreType.DMA((n * half,)),
-            pltpu.SemaphoreType.DMA((n,)),
-        ],
-        compiler_params=pltpu.CompilerParams(
-            collective_id=collective_id, has_side_effects=True, vmem_limit_bytes=56 * 1024 * 1024
-        ),
-        name="reduce_grads",
-    )(*grads)
+            self.stores.append(copy)
+
+    def step(self, t):
+        for s in range(self.stages - 1, -1, -1):
+            j = t - LAG * s
+            if 0 <= j < len(self.chunks):
+                self.stage(j, s)
+
+    def finish(self):
+        for copy, seen, left in self.started:
+            if not left:
+                copy.wait_send()
+            if not seen:
+                copy.wait_recv()
+        for copy in self.stores:
+            copy.wait()
 
 
 def nt(left, right):
@@ -469,6 +479,328 @@
         compiler_params=pltpu.CompilerParams(vmem_limit_bytes=40 * 1024 * 1024),
         name="attend_back",
     )(q, k, v, o, do, probs)
+
+
+TILE = 256
+STAGED = 3
+
+
+def tiles(count, body):
+    lax.fori_loop(0, count, lambda n, c: (body(pl.multiple_of(n * TILE, TILE)), c)[1], 0)
+
+
+class Loads:
+    def __init__(self, sem, ring, items):
+        self.sem, self.ring, self.items, self.next, self.copies = sem, ring, items, 0, {}
+
+    def start(self):
+        if self.next < len(self.items):
+            k = self.next
+            self.next += 1
+            group = []
+            for n, (src, dst) in enumerate(self.items[k](k % self.ring)):
+                copy = pltpu.make_async_copy(src, dst, self.sem.at[k % self.ring, n])
+                copy.start()
+                group.append(copy)
+            self.copies[k] = group
+
+    def wait(self, k):
+        for copy in self.copies.pop(k):
+            copy.wait()
+        return k % self.ring
+
+
+def tail_kernel(ndp, nf, shapes, chunks, scale, *refs):
+    (
+        w_down, w_up, w_out, w_qkv, slope, d_hf, unit, df1, df2, du2, dz2, dqkv2,
+        a1, a2, h1, h2, o1, o2, x1, x2, q, k, v, o, probs, sums_in, gain, inverse, entry_hot,
+    ) = refs[:29]
+    outs, g0 = refs[29:34], refs[34]
+    (
+        r_down, r_up, r_out, r_qkv, r_qkv2, lhs, turned, staged, gh, unit_v, weight, slope_v, pair_v,
+        do, probs_v, sums, w_sem, s_sem, p_sem, l_sem, m_sem,
+    ) = refs[35:56]
+    tokens, width = df1.shape
+    part = min(1024, width)
+    ff = w_down.shape[0]
+    parts = ff // part
+    wide = part // TILE
+    pair = pair_v.shape[3]
+    pairs = width // pair
+    n_mid = 3
+
+    misc = []
+    def load(src, dst):
+        copy = pltpu.make_async_copy(src, dst, m_sem.at[len(misc)])
+        copy.start()
+        misc.append(copy)
+        return copy
+
+    need_df = [load(df1, r_down.at[0]), load(df2, r_down.at[1])]
+    need_hf = [load(d_hf, gh), load(unit, unit_v)]
+    need_sums = load(sums_in, sums)
+    need_du2 = load(du2, r_up.at[1])
+    need_dz2 = load(dz2, r_out.at[1])
+    need_dqkv2 = load(dqkv2, r_qkv2)
+
+    columns = lambda t: pl.ds(t * part, part)
+    weights = Loads(w_sem, 2, (
+        [lambda s, t=t: [(w_down.at[columns(t)], weight.at[s])] for t in range(parts)]
+        + [lambda s, t=t: [(w_up.at[:, columns(t)], weight.at[s])] for t in range(parts)]
+        + [lambda s: [(w_out, weight.at[s])]]
+        + [lambda s, t=t: [(w_qkv.at[:, columns(t)], weight.at[s])] for t in range(n_mid)]
+    ))
+    slopes = Loads(s_sem, 2, [lambda s, t=t: [(slope.at[:, columns(t)], slope_v.at[s])] for t in range(parts)])
+    heads = Loads(p_sem, 2, [
+        lambda s, p=p: [(t.at[:, pl.ds(p * pair, pair)], pair_v.at[s, n]) for n, t in enumerate((q, k, v, o))]
+        + [(probs.at[pl.ds(2 * p, 2)], probs_v.at[s])]
+        for p in range(pairs)
+    ])
+    lefts = ((a1, a2), (h1, h2), (o1, o2), (x1, x2))
+
+    def left_item(j):
+        i, r0, _, rn, _, _ = chunks[j]
+
+        def item(s):
+            block = shapes[i][0] // nf
+            core = lax.rem(lax.axis_index("fsdp"), 2)
+            out = []
+            for app in range(2):
+                for n in range(nf):
+                    f = 2 * n + core if n < nf // 2 else 2 * (n - nf // 2) + 1 - core
+                    features = pl.ds(pl.multiple_of(f * block + r0, rn), rn)
+                    if rn % 128 == 0:
+                        out.append((lefts[i][app].at[:, features], lhs.at[s, app, n]))
+                    else:
+                        out.append((lefts[i][app].at[features], lhs.at[s, app, n]))
+            return out
+
+        return item
+
+    rows_of = [j for j in range(len(chunks)) if chunks[j][0] < 4]
+    left = Loads(l_sem, 2, [left_item(j) for j in rows_of])
+    rights = (
+        lambda app, at: r_down[app, :, at],
+        lambda app, at: r_up[app, :, at],
+        lambda app, at: r_out[app, :, at],
+        lambda app, at: r_qkv[:, at] if app == 0 else r_qkv2[:, at],
+    )
+
+    def source(engine, j):
+        i, r0, c0, rn, cn, _ = chunks[j]
+        slot, s = engine.slot(j), j % STAGED
+        engine.sent(("staged", s))
+        half = nf // 2
+        if i < 4:
+            buffer = left.wait(j)
+            for app in range(2):
+                for n in range(nf):
+                    block = lhs[buffer, app, n]
+                    turned[pl.ds(n * rn, rn), pl.ds(app * tokens, tokens)] = block.T if rn % 128 == 0 else block
+            left.start()
+
+            def tile(at):
+                right = pl.ds(c0 + at, TILE)
+                total = nn(turned[:, :tokens], rights[i](0, right)) + nn(turned[:, tokens:], rights[i](1, right))
+                total = total.astype(BF).reshape(nf, rn, TILE)
+                engine.held[slot, :, :, pl.ds(at, TILE)] = total[:half]
+                staged[s, :, :, pl.ds(at, TILE)] = total[half:]
+
+            tiles(cn // TILE, tile)
+        else:
+            block = sums[pl.ds(r0, rn), :].astype(BF)
+            for b in range(half):
+                engine.held[slot, b, :rn] = block
+                staged[s, b, :rn] = block
+        src = staged.at[s, :, pl.ds(0, rn), pl.ds(0, cn)]
+        dst = engine.from_core.at[j % CORE_SLOTS, :, pl.ds(0, rn), pl.ds(0, cn)]
+        return [], [engine.push(src, dst, engine.sibling, ("staged", s))]
+
+    def target(j):
+        i, r0, c0, rn, cn, _ = chunks[j]
+        return outs[i].at[pl.ds(r0, rn), pl.ds(c0, cn)]
+
+    def task_du(t):
+        def run():
+            s = weights.wait(t)
+            slopes.wait(t)
+
+            def tile(at):
+                d = nt(r_down[0], weight[s, pl.ds(at, TILE), :])
+                du = (d * slope_v[t % 2, :, pl.ds(at, TILE)].astype(F32)).astype(BF)
+                r_up[0, :, pl.ds(t * part + at, TILE)] = du
+                sums[5 + t : 6 + t, pl.ds(at, TILE)] += jnp.sum(du.astype(F32), axis=0, keepdims=True)
+
+            tiles(wide, tile)
+            weights.start()
+            slopes.start()
+        return run
+
+    def task_gh(t):
+        def run():
+            if t == 0:
+                for copy in need_hf:
+                    copy.wait()
+            s = weights.wait(parts + t)
+
+            def tile(at):
+                gh[:, pl.ds(at, TILE)] += nt(r_up[0, :, t * part : (t + 1) * part], weight[s, pl.ds(at, TILE), :])
+
+            tiles(wide, tile)
+            weights.start()
+        return run
+
+    def task_norm():
+        def tile(at):
+            rows = pl.ds(at, TILE)
+            g, u = gh[rows, :], unit_v[rows, :].astype(F32)
+            gg = g * gain[...]
+            m1 = jnp.mean(gg, axis=1, keepdims=True)
+            m2 = jnp.mean(gg * u, axis=1, keepdims=True)
+            d = (gg - m1 - u * m2) * inverse[rows, :]
+            gh[rows, :] = d
+            dz = d.astype(BF)
+            r_out[0, rows, :] = dz
+            total = lambda t: jnp.sum(t, axis=0, keepdims=True)
+            sums[2:3, :] += total(dz.astype(F32))
+            sums[3:4, :] += total(g * u)
+            sums[4:5, :] += total(g)
+
+        tiles(tokens // TILE, tile)
+        need_dz2.wait()
+
+    def task_do():
+        s = weights.wait(2 * parts)
+
+        def tile(at):
+            do[:, pl.ds(at, TILE)] = nt(r_out[0], weight[s, pl.ds(at, TILE), :]).astype(BF)
+
+        tiles(width // TILE, tile)
+        weights.start()
+
+    def task_heads(p):
+        def run():
+            s = heads.wait(p)
+            at = slice(p * pair, (p + 1) * pair)
+            dq, dk, dv = attend_back_math(
+                pair_v[s, 0], pair_v[s, 1], pair_v[s, 2], pair_v[s, 3], do[:, at], lambda h: probs_v[s, h], scale
+            )
+            r_qkv[:, at] = dq
+            r_qkv[:, width + p * pair : width + (p + 1) * pair] = dk
+            r_qkv[:, 2 * width + p * pair : 2 * width + (p + 1) * pair] = dv
+            total = lambda t: jnp.sum(t.astype(F32), axis=0, keepdims=True)
+            sums[0:1, at] += total(dq)
+            sums[1:2, at] += total(dv)
+            heads.start()
+        return run
+
+    def task_back(t):
+        def run():
+            s = weights.wait(2 * parts + 1 + t)
+
+            def tile(at):
+                gh[:, pl.ds(at, TILE)] += nt(r_qkv[:, t * part : (t + 1) * part], weight[s, pl.ds(at, TILE), :])
+
+            tiles(wide, tile)
+            weights.start()
+        return run
+
+    def task_table():
+        def tile(at):
+            g = gh[:, pl.ds(at, TILE)]
+            high = g.astype(BF)
+            rest = (g - high.astype(F32)).astype(BF)
+            sums[16:48, pl.ds(at, TILE)] += nn(entry_hot[...], high) + nn(entry_hot[...], rest)
+
+        tiles(width // TILE, tile)
+        load(gh, g0)
+
+    for _ in range(2):
+        weights.start()
+        slopes.start()
+        left.start()
+        heads.start()
+    engine = Engine(ndp, nf, chunks, refs[56:], source, target)
+    for copy in need_df:
+        copy.wait()
+    need_sums.wait()
+    counts = [sum(c[0] == i for c in chunks) for i in range(5)]
+    first = [sum(counts[:i]) for i in range(5)]
+    early = [task_du(t) for t in range(parts)] + [task_gh(t) for t in range(parts)]
+    middle = [task_norm, task_do] + [task_heads(p) for p in range(pairs)]
+    late = [task_back(t) for t in range(n_mid)] + [task_table]
+    plan = {}
+
+    def spread(tasks, begin, end):
+        for n, task in enumerate(tasks):
+            plan.setdefault(begin + n * (end - begin) // len(tasks), []).append(task)
+
+    spread(early, 0, first[1])
+    spread(middle, first[1], first[3] - 1)
+    spread(late, first[3], first[4])
+    for t in range(engine.steps):
+        if t == first[1]:
+            need_du2.wait()
+        if t == first[3]:
+            need_dqkv2.wait()
+        engine.step(t)
+        for task in plan.get(t, ()):
+            task()
+    engine.finish()
+    misc[-1].wait()
+
+
+def tail(ndp, nf, collective_id, scale, big, gain, inverse, entry_hot):
+    w_down, w_up, w_out, w_qkv = big[:4]
+    df1 = big[7]
+    tokens, width = df1.shape
+    ff = w_down.shape[0]
+    extra = big[25].shape[0]
+    shapes = (w_down.shape, w_up.shape, w_out.shape, w_qkv.shape, (nf * extra, width))
+    chunks = chunk_list(ndp, nf, shapes, KINDS)
+    half = nf // 2
+    part = min(1024, width)
+    pair = 2 * (width // HEADS)
+    rn = chunks[0][3]
+    if rn % 128:
+        big = big[:12] + [t.T for t in big[12:20]] + big[20:]
+    any_space = pl.BlockSpec(memory_space=pl.ANY)
+    vmem = pl.BlockSpec(memory_space=pltpu.VMEM)
+    return pl.pallas_call(
+        functools.partial(tail_kernel, ndp, nf, shapes, chunks, scale),
+        out_shape=[jax.ShapeDtypeStruct((r // nf, c), BF) for r, c in shapes]
+        + [jax.ShapeDtypeStruct((tokens, width), F32)],
+        in_specs=[any_space] * len(big) + [vmem] * 3,
+        out_specs=[any_space] * 6,
+        scratch_shapes=[
+            pltpu.VMEM((2, tokens, width), BF),
+            pltpu.VMEM((2, tokens, ff), BF),
+            pltpu.VMEM((2, tokens, width), BF),
+            pltpu.VMEM((tokens, 3 * width), BF),
+            pltpu.VMEM((tokens, 3 * width), BF),
+            pltpu.VMEM((2, 2, nf, tokens, rn) if rn % 128 == 0 else (2, 2, nf, rn, tokens), BF),
+            pltpu.VMEM((nf * rn, 2 * tokens), BF),
+            pltpu.VMEM((STAGED, half, rn, part), BF),
+            pltpu.VMEM((tokens, width), F32),
+            pltpu.VMEM((tokens, width), BF),
+            pltpu.VMEM((2, part, width), BF),
+            pltpu.VMEM((2, tokens, part), BF),
+            pltpu.VMEM((2, 4, tokens, pair), BF),
+            pltpu.VMEM((tokens, width), BF),
+            pltpu.VMEM((2, 2, tokens, tokens), BF),
+            pltpu.VMEM((extra, width), F32),
+            pltpu.SemaphoreType.DMA((2, 1)),
+            pltpu.SemaphoreType.DMA((2, 1)),
+            pltpu.SemaphoreType.DMA((2, 5)),
+            pltpu.SemaphoreType.DMA((2, 2 * nf)),
+            pltpu.SemaphoreType.DMA((16,)),
+        ]
+        + engine_scratch(ndp, nf, chunks),
+        compiler_params=pltpu.CompilerParams(
+            collective_id=collective_id, has_side_effects=True, vmem_limit_bytes=61 * 1024 * 1024
+        ),
+        name="tail",
+    )(*big, gain, inverse, entry_hot)
 
 
 def dot(left, right):
@@ -539,11 +871,8 @@
     dq, dk, dv = attention_back(kept["q"], kept["k"], kept["v"], kept["mixed"], d_mixed, kept["probs"])
     d_joined = jnp.concatenate([dq, dk, dv], axis=1)
     d_rows = d_xz + back_dot(d_joined, w["qkv"])
-    vectors = (
-        jnp.concatenate([total(dq), total(dv)]), total(dz), d_gain1, d_bias1,
-        total(du), total(df), d_gain2, d_bias2,
-    )
-    return d_rows, dict(df=df, du=du, dz=dz, d_joined=d_joined), vectors
+    sums = [total(dq), total(dv), total(dz), d_gain1, d_bias1, *total(du).reshape(-1, width), total(df), d_gain2, d_bias2]
+    return d_rows, dict(df=df, du=du, dz=dz, d_joined=d_joined), sums
 
 
 def shards(ndp, nf, tokens, mask_positions, mask_counts, replace_ids, cotangent, replace_table,
@@ -575,36 +904,34 @@
 
     middle, kept_one = forward(start, w, length)
     final, kept_two = forward(middle, w, length)
-    d_middle, two, vectors_two = backward(cotangent.astype(F32), kept_two, w, length)
-    d_start, one, vectors_one = backward(d_middle, kept_one, w, length)
+    d_middle, two, sums = backward(cotangent.astype(F32), kept_two, w, length)
+
+    one = kept_one
+    d_hf, d_gain2, d_bias2 = norm_back(d_middle, one["unit2"], one["inv2"], w["gain2"])
+    df = d_hf.astype(BF)
+    sums[-3:] = [sums[-3] + jnp.sum(df.astype(F32), axis=0), sums[-2] + d_gain2, sums[-1] + d_bias2]
+    sums = jnp.pad(jnp.stack(sums), ((0, 64 - len(sums)), (0, 0)))
+    entries = replace_table.shape[0]
+    entry_hot = jnp.pad(row_hot.T, ((0, 32 - entries), (0, 0)))
+    big = [
+        w["down"], w["up"], w["out"], w["qkv"], one["slope"], d_hf, one["unit1"].astype(BF),
+        df, two["df"], two["du"], two["dz"], two["d_joined"],
+        one["active"], kept_two["active"], one["hidden"], kept_two["hidden"], one["mixed"], kept_two["mixed"],
+        one["low"], kept_two["low"], one["q"], one["k"], one["v"], one["mixed"], one["probs"], sums,
+    ]
+    scale = 1.0 / math.sqrt(width // HEADS)
+    g_down, g_up, g_out, g_qkv, extra, d_start = tail(
+        ndp, nf, 1, scale, big, w["gain1"].reshape(1, width), one["inv1"], entry_hot
+    )
     token_grad = d_start * keep
-
-    def weight(left, right):
-        both = lambda a, b: jnp.concatenate([a, b], axis=0)
-        return outer_dot(both(kept_one[left], kept_two[left]), both(one[right], two[right])).astype(BF)
-
-    high = d_start.astype(BF)
-    rest = d_start - high.astype(F32)
-    mid = rest.astype(BF)
-    d_table = outer_dot(row_hot, high) + outer_dot(row_hot, mid)
-    table_rows = -(-replace_table.shape[0] // 16) * 16
-    d_table = jnp.pad(d_table, ((0, table_rows - d_table.shape[0]), (0, 0))).astype(BF)
-    vec = [a + b for a, b in zip(vectors_one, vectors_two)]
-    pieces = jnp.concatenate([t.reshape(nf, -1) for t in vec], axis=1)
-    vec_rows = 64 - table_rows
-    pieces = jnp.pad(pieces, ((0, 0), (0, vec_rows * width - count))).astype(BF).reshape(nf, vec_rows, width)
-    extra = jnp.concatenate([pieces, jnp.broadcast_to(d_table[None], (nf,) + d_table.shape)], axis=1).reshape(-1, width)
-    g_down, g_up, g_out, g_qkv, g_extra = reduce_grads(
-        ndp, nf, 1, [weight("active", "df"), weight("hidden", "du"), weight("mixed", "dz"), weight("low", "d_joined"), extra]
-    )
-    table_grad = g_extra[vec_rows : vec_rows + replace_table.shape[0]].astype(F32)
-    flat = g_extra[:vec_rows].reshape(-1).astype(F32)
-    v = []
-    at = 0
-    for size in lengths:
-        v.append(flat[at : at + size])
-        at += size
     up32 = lambda t: t.astype(F32)
+    extra = up32(extra)
+    table_grad = extra[16 : 16 + entries]
+    place = lax.axis_index("fsdp")
+    mine = lambda t: lax.dynamic_slice_in_dim(t, place * (t.shape[0] // nf), t.shape[0] // nf)
+    grown = w_up.shape[1] // width
+    v = [mine(extra[:2].reshape(-1))] + [mine(extra[n]) for n in (2, 3, 4)]
+    v += [mine(extra[5 : 5 + grown].reshape(-1))] + [mine(extra[n + grown]) for n in (5, 6, 7)]
     return (
         final.astype(BF), token_grad, table_grad, up32(g_qkv), v[0], up32(g_out), v[1], v[2], v[3],
         up32(g_up), v[4], up32(g_down), v[5], v[6], v[7],

time: 509 us -> 439 us (0.86)
  matrix products: 146 us -> 77.5 us
    dot_general x7 -> x1, matrix products: 37.9 us -> 0.26 us  [outer_dot(): lax.dot_general(left, right, (((0,), (0,)), ((), ())), preferred_element_...]
    dot_general x8 -> x4, matrix products: 65.9 us -> 29.9 us  [back_dot(): lax.dot_general(left, right, (((1,), (1,)), ((), ())), preferred_element_...]
    pallas_call x2 -> x1, Pallas kernels: 26.7 us -> 13.4 us  [attention_back(): pl.pallas_call(functools.partial(attend_back_kernel, scale), grid=(HEADS...]
    pallas_call x1, Pallas kernels: 182 us -> 192 us  [tail(): pl.pallas_call(functools.partial(tail_kernel, ndp, nf, shapes, chunks, sc...]
    reduce_sum x7 -> x4, other arithmetic: 11.9 us -> 6.01 us  [backward(): total = lambda t: jnp.sum(t.astype(F32), axis=0)]
    unnamed x150 -> x111, local copies, waits for them, and re-layouts: 19.3 us -> 17.8 us
where the time goes in v3:
time: 439 us; the launch traced here: 431 us
  Pallas kernels  297 us (68%)
  matrix products  77.5 us (18%)
  other arithmetic  27.5 us (6%)
  local copies, waits for them, and re-layouts  26.7 us (6%)
    pallas_call x1, Pallas kernels, tail(): pl.pallas_call(functools.partial(tail_kernel, ndp, nf, shapes, chunks, sc...  192 us
    pallas_call x1, Pallas kernels, gather_weights(): pl.pallas_call(functools.partial(gather_kernel, ndp, nf, shapes), out_sha...  68.4 us
    dot_general x9, matrix products, dot(): return jnp.dot(left, right, preferred_element_type=F32)  47.3 us
    dot_general x4, matrix products, back_dot(): lax.dot_general(left, right, (((1,), (1,)), ((), ())), preferred_element_...  29.9 us
    pallas_call x2, Pallas kernels, attention(): pl.pallas_call(attend_kernel, grid=(HEADS // 2,), in_specs=[cols] * 3, ou...  22.6 us
    unnamed x111, local copies, waits for them, and re-layouts  17.8 us
    pallas_call x1, Pallas kernels, attention_back(): pl.pallas_call(functools.partial(attend_back_kernel, scale), grid=(HEADS...  13.4 us
    convert_element_type x5, other arithmetic, shards(): up32 = lambda t: t.astype(F32)  9.86 us

profile of v3, /device:TPU:0, one launch (start us, length us, event | category | flops | bytes accessed | tf_op | source)
XLA Modules:
  0.0 430.9 jit_solution(5767359128462478393)
XLA Ops:
  7.4 1.6 copy-done.12
  9.0 1.6 copy-done.13
  10.6 1.4 copy-done.14
  13.0 68.4 %gather_weights.1 = (bf16[1024,3072]{1,0:T(8,128)(2,1)S(1)}, bf16[1024,1024]{1,0:T(8,128)(2,1)S(1)}, bf16[1024,4096]{1,0:T(8,128)(2,1)}, bf16[4096,1024]{1,0:T(8,128)(2,1)}, bf16[4,16,256]{2,1,0:T(8,128)(2,1)S(1)}) custom-call(bf16[256,3072]{1,0:T(8,128)(2,1)S(1)} %copy-done.14, bf16[256,1024]{1,0:T(8,128)(2,1)S(1)} %copy-done.15, ...), custom_call_target="tpu_custom_call" | custom-call | tf_op jit(solution)/shard_map/gather_weights/pallas_call | solution.py:169
  82.7 2.3 fusion.35
  84.9 3.4 fusion.40
  89.2 11.2 %attend.2 = (bf16[512,1024]{1,0:T(8,128)(2,1)S(1)}, bf16[16,512,512]{2,1,0:T(8,128)(2,1)S(1)}) custom-call(bf16[512,1024]{1,0:T(8,128)(2,1)S(1)} %get-tuple-element.76.q_ref.refs_20_, bf16[512,1024]{1,0:T(8,128)(2,1)S(1)} %slice.173.k_ref.refs_21_, bf16[512,1024]{1,0:T(8,128)(2,1)S(1)} %get-tuple-element.75.v_ref.refs_22_), custom_call_target="tpu_custom_call" | custom-call | tf_op jit(solution)/shard_map/attend/pallas_call | solution.py:429
  100.5 4.5 %fusion.36 = (f32[512]{0:T(512)S(1)}, f32[512,1024]{1,0:T(8,128)S(1)}) fusion(f32[512,1024]{1,0:T(8,128)} %get-tuple-element.100, f32[1024]{0:T(1024)S(1)} %bitcast.149, bf16[512,1024]{1,0:T(8,128)(2,1)S(1)} %get-tuple-element.35.refs_16_.refs_23_, bf16[1024,1024]{1,0:T(8,128)(2,1)S(1)} %get-tuple-element.36.refs_2_), kind=kOutput, calls=%fused_computation.132 | convolution fusion | flops 1075314176 | bytes 7346176 | tf_op jit(solution)/shard_map/dot_general | solution.py:807
  105.4 1.4 multiply_convert_fusion.3
  106.8 12.2 %fusion.4 = (bf16[512,4096]{1,0:T(8,128)(2,1)}, bf16[512,4096]{1,0:T(8,128)(2,1)S(1)}) fusion(f32[4096]{0:T(1024)S(1)} %bitcast.137, bf16[512,1024]{1,0:T(8,128)(2,1)S(1)} %get-tuple-element.79.refs_14_, bf16[1024,4096]{1,0:T(8,128)(2,1)} %get-tuple-element.37.refs_1_), kind=kOutput, calls=%fused_computation.6 | convolution fusion | flops 4320133120 | bytes 17842176 | tf_op jit(solution)/shard_map/dot_general | solution.py:807
  119.1 4.8 %fusion.37 = (f32[512]{0:T(512)S(1)}, f32[512,1024]{1,0:T(8,128)S(1)}) fusion(f32[1024]{0:T(1024)S(1)} %bitcast.147, bf16[512,4096]{1,0:T(8,128)(2,1)S(1)} %get-tuple-element.72.refs_12_, bf16[4096,1024]{1,0:T(8,128)(2,1)S(1)} %bitcast.97, f32[1024]{0:T(1024)S(1)} %bitcast.118, f32[1024]{0:T(1024)S(1)} %bitcast.112, f32[512]{0:T(512)S(1)} %add_rsqrt_fusion.3, ...), kind=kOutput, calls=%fused_computation.133 | convolution fusion | flops 4298636800 | bytes 16795648 | tf_op jit(solution)/shard_map/dot_general | solution.py:807
  124.7 3.4 fusion.41
  128.9 11.4 %attend.3 = (bf16[512,1024]{1,0:T(8,128)(2,1)S(1)}, bf16[16,512,512]{2,1,0:T(8,128)(2,1)S(1)}) custom-call(bf16[512,1024]{1,0:T(8,128)(2,1)S(1)} %get-tuple-element.74.q_ref, bf16[512,1024]{1,0:T(8,128)(2,1)S(1)} %slice.172.k_ref, bf16[512,1024]{1,0:T(8,128)(2,1)S(1)} %get-tuple-element.73.v_ref), custom_call_target="tpu_custom_call" | custom-call | tf_op jit(solution)/shard_map/attend/pallas_call | solution.py:429
  140.3 1.5 fusion.38
  141.8 1.7 copy-done.5
  144.3 10.4 %multiply_convert_fusion.1 = (bf16[512,4096]{1,0:T(8,128)(2,1)S(1)}, f32[512,4096]{1,0:T(8,128)}) fusion(f32[4096]{0:T(1024)S(1)} %bitcast.138, bf16[512,1024]{1,0:T(8,128)(2,1)S(1)} %fusion.24.refs_15_, bf16[1024,4096]{1,0:T(8,128)(2,1)} %get-tuple-element.37.refs_1_), kind=kOutput, calls=%fused_computation.14 | convolution fusion | flops 4307550208 | bytes 22036480 | tf_op jit(solution)/shard_map/dot_general | solution.py:807
  154.8 4.8 %fusion.39 = (f32[512]{0:T(512)S(1)}, f32[512,1024]{1,0:T(8,128)S(1)}) fusion(f32[1024]{0:T(1024)S(1)} %bitcast.148, bf16[512,4096]{1,0:T(8,128)(2,1)S(1)} %get-tuple-element.107.refs_13_, bf16[4096,1024]{1,0:T(8,128)(2,1)S(1)} %bitcast.99, f32[1024]{0:T(1024)S(1)} %bitcast.120, f32[1024]{0:T(1024)S(1)} %bitcast.114, f32[512]{0:T(512)S(1)} %add_rsqrt_fusion.1, ...), kind=kOutput, calls=%fused_computation.135 | convolution fusion | flops 4298636800 | bytes 16795648 | tf_op jit(solution)/shard_map/dot_general | solution.py:807
  159.9 1.6 copy-done.30
  162.5 1.9 convert_reduce_fusion.3
  164.4 12.8 %convert_reduce_fusion = (f32[4096]{0:T(1024)S(1)}, bf16[512,4096]{1,0:T(8,128)(2,1)}) fusion(f32[512,4096]{1,0:T(8,128)} %get-tuple-element.108, f32[4096]{0:T(1024)S(1)} %bitcast.139, bf16[512,1024]{1,0:T(8,128)(2,1)S(1)} %get-tuple-element.67.refs_8_, bf16[4096,1024]{1,0:T(8,128)(2,1)} %get-tuple-element.38.refs_0_), kind=kOutput, calls=%fused_computation.12 | convolution fusion | flops 4326420480 | bytes 22052864 | tf_op jit(solution)/shard_map/dot_general | solution.py:811
  177.2 11.9 %multiply_reduce_fusion.1 = (f32[1024]{0:T(1024)S(1)}, f32[512]{0:T(512)S(1)}, f32[512]{0:T(512)S(1)}, f32[1024]{0:T(1024)S(1)}, f32[512,1024]{1,0:T(8,128)}) fusion(f32[512,1024]{1,0:T(8,128)S(1)} %copy-done.19, f32[512]{0:T(512)S(1)} %add_rsqrt_fusion.1, f32[512]{0:T(512)S(1)} %broadcast_multiply_fusion.8, f32[1024]{0:T(1024)S(1)} %bitcast.115, ...), kind=kOutput, calls=%fused_computation.43 | convolution fusion | flops 4304401408 | bytes 19955712 | tf_op jit(solution)/shard_map/dot_general | solution.py:811
  189.1 3.8 convert_reduce_fusion.4
  192.9 1.3 convolution_convert_fusion.do_ref
  194.2 13.4 %attend_back.1 = (bf16[512,1024]{1,0:T(8,128)(2,1)S(1)}, bf16[512,1024]{1,0:T(8,128)(2,1)S(1)}, bf16[512,1024]{1,0:T(8,128)(2,1)S(1)}) custom-call(bf16[512,1024]{1,0:T(8,128)(2,1)S(1)} %get-tuple-element.74.q_ref, bf16[512,1024]{1,0:T(8,128)(2,1)S(1)} %slice.172.k_ref, bf16[512,1024]{1,0:T(8,128)(2,1)S(1)} %get-tuple-element.73.v_ref, ...), custom_call_target="tpu_custom_call" | custom-call | tf_op jit(solution)/shard_map/attend_back/pallas_call | solution.py:473
  207.8 1.4 copy-done.17
  209.9 4.0 multiply_reduce_fusion
  213.9 2.4 convert_reduce_fusion.2
  219.6 192.3 %tail.1 = (bf16[1024,1024]{1,0:T(8,128)(2,1)}, bf16[256,4096]{1,0:T(8,128)(2,1)}, bf16[256,1024]{1,0:T(8,128)(2,1)}, bf16[256,3072]{1,0:T(8,128)(2,1)}, bf16[64,1024]{1,0:T(8,128)(2,1)}, /*index=5*/f32[512,1024]{1,0:T(8,128)}) custom-call(bf16[4096,1024]{1,0:T(8,128)(2,1)} %get-tuple-element.38.refs_0_, bf16[1024,4096]{1,0:T(8,128)(2,1)} %get-tuple-element.37.refs_1_, ...), custom_call_target="tpu_custom_call" | custom-call | tf_op jit(solution)/shard_map/tail/pallas_call | solution.py:769
  411.9 3.2 broadcast_multiply_fusion
  415.8 2.0 convert_element_type.259
  421.4 4.2 convert_element_type.261
  426.2 2.5 convert_element_type.262
  (165 shorter events, 23.7 us)
Async XLA Ops:
  0.6 82.0 %copy-start = (bf16[30,1024]{1,0:T(8,128)(2,1)S(1)}, bf16[30,1024]{1,0:T(8,128)(2,1)}, u32[]{:S(2)}) copy-start(bf16[30,1024]{1,0:T(8,128)(2,1)} %param.23) | copy-start | bytes 184324
  13.0 69.2 %copy-start.37 = (s32[1,80]{1,0:T(1,128)S(1)}, s32[1,80]{1,0:T(1,128)}, u32[]{:S(2)}) copy-start(s32[1,80]{1,0:T(1,128)} %param.19) | copy-start | bytes 964
  13.0 69.2 %copy-start.38 = (s32[1,80]{1,0:T(1,128)S(1)}, s32[1,80]{1,0:T(1,128)}, u32[]{:S(2)}) copy-start(s32[1,80]{1,0:T(1,128)} %param.21) | copy-start | bytes 964
  13.0 69.6 %copy-start.34 = (bf16[512,1024]{1,0:T(8,128)(2,1)S(1)}, bf16[512,1024]{1,0:T(8,128)(2,1)}, u32[]{:S(2)}) copy-start(bf16[512,1024]{1,0:T(8,128)(2,1)} %param.18) | copy-start | bytes 3145732
  81.5 58.9 %copy-start.10 = (bf16[1024,1024]{1,0:T(8,128)(2,1)}, bf16[1024,1024]{1,0:T(8,128)(2,1)S(1)}, u32[]{:S(2)}) copy-start(bf16[1024,1024]{1,0:T(8,128)(2,1)S(1)} %get-tuple-element.36.refs_2_) | copy-start | bytes 6291460
  81.5 126.4 %copy-start.7 = (bf16[1024,3072]{1,0:T(8,128)(2,1)}, bf16[1024,3072]{1,0:T(8,128)(2,1)S(1)}, u32[]{:S(2)}) copy-start(bf16[1024,3072]{1,0:T(8,128)(2,1)S(1)} %get-tuple-element.33.refs_3_) | copy-start | bytes 18874372
  84.9 3.4 copy-start.26
  89.0 11.4 %copy-start.3 = (bf16[512,1024]{1,0:T(8,128)(2,1)}, bf16[512,1024]{1,0:T(8,128)(2,1)S(1)}, u32[]{:S(2)}) copy-start(bf16[512,1024]{1,0:T(8,128)(2,1)S(1)} %get-tuple-element.75.v_ref.refs_22_) | copy-start | bytes 3145732
  89.0 11.4 %copy-start.4 = (bf16[512,1024]{1,0:T(8,128)(2,1)}, bf16[512,1024]{1,0:T(8,128)(2,1)S(1)}, u32[]{:S(2)}) copy-start(bf16[512,1024]{1,0:T(8,128)(2,1)S(1)} %get-tuple-element.76.q_ref.refs_20_) | copy-start | bytes 3145732
  89.2 15.8 %copy-start.2 = (bf16[512,1024]{1,0:T(8,128)(2,1)}, bf16[512,1024]{1,0:T(8,128)(2,1)S(1)}, u32[]{:S(2)}) copy-start(bf16[512,1024]{1,0:T(8,128)(2,1)S(1)} %slice.173.k_ref.refs_21_) | copy-start | bytes 3145732
  100.4 4.5 %copy-start.6 = (bf16[16,512,512]{2,1,0:T(8,128)(2,1)}, bf16[16,512,512]{2,1,0:T(8,128)(2,1)S(1)}, u32[]{:S(2)}) copy-start(bf16[16,512,512]{2,1,0:T(8,128)(2,1)S(1)} %get-tuple-element.44.refs_24_) | copy-start | bytes 25165828
  100.4 4.5 %copy-start.8 = (bf16[512,1024]{1,0:T(8,128)(2,1)}, bf16[512,1024]{1,0:T(8,128)(2,1)S(1)}, u32[]{:S(2)}) copy-start(bf16[512,1024]{1,0:T(8,128)(2,1)S(1)} %get-tuple-element.35.refs_16_.refs_23_) | copy-start | bytes 3145732
  105.4 13.7 %slice-start = ((s8[8388608]{0:T(1024)(128)(4,1)}), s8[4194304]{0:T(1024)(128)(4,1)S(1)}, s32[]{:S(2)}) async-start(s8[8388608]{0:T(1024)(128)(4,1)} %bitcast.96), calls=%async_computation | async-start | bytes 8388608
  106.8 12.3 %copy-start.22 = (bf16[512,1024]{1,0:T(8,128)(2,1)}, bf16[512,1024]{1,0:T(8,128)(2,1)S(1)}, u32[]{:S(2)}) copy-start(bf16[512,1024]{1,0:T(8,128)(2,1)S(1)} %get-tuple-element.79.refs_14_) | copy-start | bytes 3145732
  106.8 12.3 %slice-start.1 = ((s8[8388608]{0:T(1024)(128)(4,1)}), s8[4194304]{0:T(1024)(128)(4,1)S(1)}, s32[]{:S(2)}) async-start(s8[8388608]{0:T(1024)(128)(4,1)} %bitcast.96), calls=%async_computation.1 | async-start | bytes 8388608
  119.1 4.8 %copy-start.28 = (bf16[512,4096]{1,0:T(8,128)(2,1)}, bf16[512,4096]{1,0:T(8,128)(2,1)S(1)}, u32[]{:S(2)}) copy-start(bf16[512,4096]{1,0:T(8,128)(2,1)S(1)} %get-tuple-element.72.refs_12_) | copy-start | bytes 12582916
  123.9 16.5 %copy-start.16 = (f32[512,1024]{1,0:T(8,128)}, f32[512,1024]{1,0:T(8,128)S(1)}, u32[]{:S(2)}) copy-start(f32[512,1024]{1,0:T(8,128)S(1)} %get-tuple-element.104) | copy-start | bytes 6291460
  124.7 3.4 copy-start.24
  140.3 53.9 %copy-start.9 = (bf16[512,1024]{1,0:T(8,128)(2,1)}, bf16[512,1024]{1,0:T(8,128)(2,1)S(1)}, u32[]{:S(2)}) copy-start(bf16[512,1024]{1,0:T(8,128)(2,1)S(1)} %get-tuple-element.39.o_ref.refs_17_) | copy-start | bytes 3145732
  143.5 11.2 %copy-start.18 = (f32[512,1024]{1,0:T(8,128)}, f32[512,1024]{1,0:T(8,128)S(1)}, u32[]{:S(2)}) copy-start(f32[512,1024]{1,0:T(8,128)S(1)} %get-tuple-element.106) | copy-start | bytes 6291460
  143.9 10.9 %slice-start.2 = ((s8[8388608]{0:T(1024)(128)(4,1)}), s8[4194304]{0:T(1024)(128)(4,1)S(1)}, s32[]{:S(2)}) async-start(s8[8388608]{0:T(1024)(128)(4,1)} %bitcast.98), calls=%async_computation.2 | async-start | bytes 8388608
  144.3 10.4 %copy-start.25 = (bf16[512,1024]{1,0:T(8,128)(2,1)}, bf16[512,1024]{1,0:T(8,128)(2,1)S(1)}, u32[]{:S(2)}) copy-start(bf16[512,1024]{1,0:T(8,128)(2,1)S(1)} %fusion.24.refs_15_) | copy-start | bytes 3145732
  144.3 10.4 %slice-start.3 = ((s8[8388608]{0:T(1024)(128)(4,1)}), s8[4194304]{0:T(1024)(128)(4,1)S(1)}, s32[]{:S(2)}) async-start(s8[8388608]{0:T(1024)(128)(4,1)} %bitcast.98), calls=%async_computation.3 | async-start | bytes 8388608
  154.7 4.8 %copy-start.29 = (bf16[512,4096]{1,0:T(8,128)(2,1)}, bf16[512,4096]{1,0:T(8,128)(2,1)S(1)}, u32[]{:S(2)}) copy-start(bf16[512,4096]{1,0:T(8,128)(2,1)S(1)} %get-tuple-element.107.refs_13_) | copy-start | bytes 12582916
  159.6 4.9 %copy-start.20 = (f32[512,1024]{1,0:T(8,128)}, f32[512,1024]{1,0:T(8,128)S(1)}, u32[]{:S(2)}) copy-start(f32[512,1024]{1,0:T(8,128)S(1)} %get-tuple-element.110) | copy-start | bytes 6291460
  164.4 12.8 %copy-start.27 = (bf16[512,1024]{1,0:T(8,128)(2,1)}, bf16[512,1024]{1,0:T(8,128)(2,1)S(1)}, u32[]{:S(2)}) copy-start(bf16[512,1024]{1,0:T(8,128)(2,1)S(1)} %get-tuple-element.67.refs_8_) | copy-start | bytes 3145732
  164.4 12.8 %copy-start.19 = (f32[512,1024]{1,0:T(8,128)S(1)}, f32[512,1024]{1,0:T(8,128)}, u32[]{:S(2)}) copy-start(f32[512,1024]{1,0:T(8,128)} %copy-done.18) | copy-start | bytes 6291460
  189.1 3.8 copy-start.11
  209.9 4.0 copy-start.21
  411.9 3.9 copy-start.33
  421.4 4.9 %copy-start.31 = (bf16[1024,1024]{1,0:T(8,128)(2,1)S(1)}, bf16[1024,1024]{1,0:T(8,128)(2,1)}, u32[]{:S(2)}) copy-start(bf16[1024,1024]{1,0:T(8,128)(2,1)} %get-tuple-element.50) | copy-start | bytes 6291460
  426.2 4.2 copy-start.1
  (11 other events, 21.9 us)
